TPU v7x, 256 devices: a whole 4x4x8 slice. The times are simulated.
256 devices in a mesh: dp: 16 (over x_hi, z), ctx: 16 (over x_lo, y, core).
Axes of the slice: x: 4 (x_hi: 2, x_lo: 2; x = x_hi * 2 + x_lo), y: 4, z: 8, core: 2. Of those that a mesh axis runs over, the one named last changes fastest.
Arguments:
- events: bfloat16 [65536, 1024], P(('dp', 'ctx')), may hold values from -6 to 6
- w_in: bfloat16 [1024, 4096], replicated, may hold values from -0.1875 to 0.1875
- w_out: bfloat16 [1024, 1024], replicated, may hold values from -0.1875 to 0.1875
- targets: bfloat16 [65536, 1024], P(('dp', 'ctx')), may hold values from -12 to 12
- target_ids: int32 [65536], P(('dp', 'ctx')), may hold values from 0 to 63
- lengths: int32 [16, 4], P('dp'), may hold values from 1 to 2048, 4096 in all within a row
- block_order: int32 [16, 16], P('dp'), may hold values from 0 to 15, each once within a row
- negatives: bfloat16 [2048, 1024], P('dp'), may hold values from -12 to 12
- neg_ids: int32 [2048], replicated, may hold values from 0 to 63
Outputs:
- event_loss: float32 [65536], P(('dp', 'ctx'))
- neg_grad: float32 [2048, 1024], P(('dp', 'ctx'))
Inputs may be any that keep to these rules, and one draw needn't show every extreme that they name: `lengths`: each row sums to 4096; its largest entry is exactly 2048. `block_order`: each row holds every number below 16 once.
All inputs are finite; a program needn't handle non-finite values.
Results may differ from a plain program's by a relative error of at most 0.011.
Values may be sent and summed in bfloat16 or wider, within the bound.
A program may use at most 64 MiB of HBM per device.

v0:
```python
import math

import jax
import jax.numpy as jnp
from jax import lax
from jax.sharding import PartitionSpec as P

HEADS = 8


def passed_along(value, axis, steps):
    count = lax.axis_size(axis)
    pairs = [(source, (source + steps) % count) for source in range(count)]
    return lax.ppermute(value, axis, pairs)


def layer_norm(values):
    center = values - jnp.mean(values, axis=-1, keepdims=True)
    spread = jnp.mean(center * center, axis=-1, keepdims=True)
    return center * lax.rsqrt(spread + 1e-05)


def shards(events, w_in, w_out, targets, target_ids, lengths, block_order, negatives, neg_ids):
    tok_rows, feat_width = events.shape
    head_count = HEADS
    head_size = feat_width // head_count
    cycle_size = lax.axis_size("ctx")
    my_slot = lax.axis_index("ctx")
    slot_blocks = block_order[0]
    user_lens = lengths[0]
    user_count = user_lens.shape[0]
    user_ends = jnp.cumsum(user_lens)
    row_index = jnp.arange(tok_rows, dtype=jnp.int32)
    scale = 1.0 / math.sqrt(feat_width)
    normed = layer_norm(events.astype(jnp.float32)).astype(jnp.bfloat16)
    projected = jax.nn.silu(jnp.dot(normed, w_in, preferred_element_type=jnp.float32)).astype(
        jnp.bfloat16
    )
    gate_rows = projected[:, :feat_width]
    value_rows = projected[:, feat_width : 2 * feat_width]
    query_rows = projected[:, 2 * feat_width : 3 * feat_width]
    key_rows = projected[:, 3 * feat_width :]
    my_block = slot_blocks[my_slot]

    def locate(key_block):
        positions = key_block * tok_rows + row_index
        user_ids = jnp.sum((positions[:, None] >= user_ends[None, :]).astype(jnp.int32), axis=1)
        return (positions, user_ids)

    query_pos, query_user = locate(my_block)
    user_size = jnp.sum(
        jnp.where(
            query_user[:, None] == jnp.arange(user_count, dtype=jnp.int32)[None, :],
            user_lens[None, :],
            0,
        ),
        axis=1,
    ).astype(jnp.float32)
    queries = query_rows.reshape(tok_rows, head_count, head_size)

    def add_tile(running, query_part, key_value, key_block):
        key_pos, key_user = locate(key_block)
        visible = (query_user[:, None] == key_user[None, :]) & (
            key_pos[None, :] <= query_pos[:, None]
        )
        part_heads = query_part.shape[1]
        key_part = key_value[0].reshape(tok_rows, part_heads, head_size)
        value_part = key_value[1].reshape(tok_rows, part_heads, head_size)
        scores = jnp.einsum(
            "qhd,khd->hqk", query_part, key_part, preferred_element_type=jnp.float32
        ) / math.sqrt(head_size)
        weights = (
            jnp.where(visible[None], jax.nn.silu(scores), 0.0) / user_size[None, :, None]
        ).astype(jnp.bfloat16)
        return running + jnp.einsum(
            "hqk,khd->qhd", weights, value_part, preferred_element_type=jnp.float32
        )

    def maybe_tile(running, query_part, key_value, key_block):
        return lax.cond(
            key_block <= my_block,
            lambda: add_tile(running, query_part, key_value, key_block),
            lambda: running,
        )

    key_value = jnp.stack([key_rows, value_rows])
    running = maybe_tile(
        jnp.zeros((tok_rows, head_count, head_size), jnp.float32), queries, key_value, my_block
    )

    def cycle_step(step_index, carry):
        running, moving = carry
        moving = passed_along(moving, "ctx", 1)
        key_block = slot_blocks[(my_slot - step_index) % cycle_size]
        return (maybe_tile(running, queries, moving, key_block), moving)

    running, key_value = lax.fori_loop(1, cycle_size, cycle_step, (running, key_value))
    attended = running.reshape(tok_rows, feat_width)
    mixed = (layer_norm(attended) * gate_rows.astype(jnp.float32)).astype(jnp.bfloat16)
    user_vec = (
        events.astype(jnp.float32) + jnp.dot(mixed, w_out, preferred_element_type=jnp.float32)
    ).astype(jnp.bfloat16)
    pos_logit = jnp.sum(user_vec.astype(jnp.float32) * targets.astype(jnp.float32), axis=-1) * scale
    all_negatives = lax.all_gather(negatives, "dp", axis=0, tiled=True)
    logits = (
        jnp.einsum("ed,nd->en", user_vec, all_negatives, preferred_element_type=jnp.float32) * scale
    )
    allowed = target_ids[:, None] != neg_ids[None, :]
    row_top = jnp.maximum(
        pos_logit, jnp.max(jnp.where(allowed, logits, pos_logit[:, None]), axis=1)
    )
    denominator = jnp.exp(pos_logit - row_top) + jnp.sum(
        jnp.where(allowed, jnp.exp(logits - row_top[:, None]), 0.0), axis=1
    )
    log_total = row_top + jnp.log(denominator)
    event_loss = log_total - pos_logit
    sample_prob = jnp.where(allowed, jnp.exp(logits - log_total[:, None]), 0.0).astype(jnp.bfloat16)
    local_grad = (
        jnp.einsum("en,ed->nd", sample_prob, user_vec, preferred_element_type=jnp.float32) * scale
    )
    neg_grad = lax.psum_scatter(local_grad, ("dp", "ctx"), scatter_dimension=0, tiled=True)
    return (event_loss, neg_grad)


def solution(mesh):
    return jax.shard_map(
        shards,
        mesh=mesh,
        in_specs=(
            P(("dp", "ctx"), None),
            P(),
            P(),
            P(("dp", "ctx"), None),
            P(("dp", "ctx")),
            P("dp", None),
            P("dp", None),
            P("dp", None),
            P(),
        ),
        out_specs=(P(("dp", "ctx")), P(("dp", "ctx"), None)),
        check_vma=False,
    )
```

profile of v0, /device:TPU:24, one launch (start us, length us, event | category | flops | bytes accessed | tf_op | source)
XLA Modules:
  0.0 1674.9 jit_solution(6428522997401512184)
XLA Ops:
  8.0 1.2 convert_reduce_fusion.1
  9.2 1.3 fusion.19
  10.5 6.1 multiply_convert_fusion
  16.7 1.8 slice_bitcast_fusion.1
  18.5 1.0 copy.37
  22.1 3.4 convolution_bitcast_fusion.1
  25.5 2.6 copy.31
  28.1 1.3 pad_maximum_fusion
  29.4 1.3 copy.32
  30.7 319.2 %while.21 = (s32[]{:T(128)}, f32[256,8,128]{2,0,1:T(8,128)}, bf16[2,256,1024]{1,2,0:T(8,128)(2,1)}, s32[]{:T(128)}, s32[16]{0:T(128)S(1)}, /*index=5*/s32[]{:T(1...) while((s32[]{:T(128)}, f32[256,8,128]{2,0,1:T(8,128)}, ...), condition=%wide.region_9.10_spmd.clone, body=%wide.region_5.9_spmd.clone.sunk | while | flops 273091872 | bytes 12202470 | solution.py:97
  32.5 12.6 collective-permute-done
  45.1 1.0 copy.64
  46.1 4.7 collective-permute-start
  52.6 11.4 collective-permute-done
  64.0 5.8 conditional.3
  64.0 1.1 fusion.54
  65.9 3.9 fusion.4
  69.8 1.0 copy.64
  70.8 4.1 collective-permute-start
  76.7 8.5 collective-permute-done
  85.2 1.0 copy.64
  86.2 21.7 %collective-permute-start = (bf16[2,256,1024]{1,2,0:T(8,128)(2,1)}, bf16[2,256,1024]{1,2,0:T(8,128)(2,1)S(1)}, u32[]{:S(2)}, u32[]{:S(2)}) collective-permute-start(bf16[2,256,1024]{1,2,0:T(8,128)(2,1)} %get-tuple-element.511), channel_id=1, source_target_pairs={{0,1},{1,2},{2,3},{3,4},{4,5},{5,6},{6,7},{7,8},{8,9},{9,10},{10,1... | collective-permute-start | bytes 3145736 | tf_op jit(solution)/shard_map/while/body/eval_jaxpr/ppermute | solution.py:14
  110.4 1.0 copy.64
  111.4 19.9 %collective-permute-start = (bf16[2,256,1024]{1,2,0:T(8,128)(2,1)}, bf16[2,256,1024]{1,2,0:T(8,128)(2,1)S(1)}, u32[]{:S(2)}, u32[]{:S(2)}) collective-permute-start(bf16[2,256,1024]{1,2,0:T(8,128)(2,1)} %get-tuple-element.511), channel_id=1, source_target_pairs={{0,1},{1,2},{2,3},{3,4},{4,5},{5,6},{6,7},{7,8},{8,9},{9,10},{10,1... | collective-permute-start | bytes 3145736 | tf_op jit(solution)/shard_map/while/body/eval_jaxpr/ppermute | solution.py:14
  133.7 1.0 copy.64
  134.7 14.0 collective-permute-start
  152.2 25.7 %collective-permute-start = (bf16[2,256,1024]{1,2,0:T(8,128)(2,1)}, bf16[2,256,1024]{1,2,0:T(8,128)(2,1)S(1)}, u32[]{:S(2)}, u32[]{:S(2)}) collective-permute-start(bf16[2,256,1024]{1,2,0:T(8,128)(2,1)} %get-tuple-element.511), channel_id=1, source_target_pairs={{0,1},{1,2},{2,3},{3,4},{4,5},{5,6},{6,7},{7,8},{8,9},{9,10},{10,1... | collective-permute-start | bytes 3145736 | tf_op jit(solution)/shard_map/while/body/eval_jaxpr/ppermute | solution.py:14
  180.4 1.0 copy.64
  181.4 15.4 collective-permute-start
  199.3 1.0 copy.64
  200.2 19.9 %collective-permute-start = (bf16[2,256,1024]{1,2,0:T(8,128)(2,1)}, bf16[2,256,1024]{1,2,0:T(8,128)(2,1)S(1)}, u32[]{:S(2)}, u32[]{:S(2)}) collective-permute-start(bf16[2,256,1024]{1,2,0:T(8,128)(2,1)} %get-tuple-element.511), channel_id=1, source_target_pairs={{0,1},{1,2},{2,3},{3,4},{4,5},{5,6},{6,7},{7,8},{8,9},{9,10},{10,1... | collective-permute-start | bytes 3145736 | tf_op jit(solution)/shard_map/while/body/eval_jaxpr/ppermute | solution.py:14
  223.6 14.0 collective-permute-start
  241.1 19.9 %collective-permute-start = (bf16[2,256,1024]{1,2,0:T(8,128)(2,1)}, bf16[2,256,1024]{1,2,0:T(8,128)(2,1)S(1)}, u32[]{:S(2)}, u32[]{:S(2)}) collective-permute-start(bf16[2,256,1024]{1,2,0:T(8,128)(2,1)} %get-tuple-element.511), channel_id=1, source_target_pairs={{0,1},{1,2},{2,3},{3,4},{4,5},{5,6},{6,7},{7,8},{8,9},{9,10},{10,1... | collective-permute-start | bytes 3145736 | tf_op jit(solution)/shard_map/while/body/eval_jaxpr/ppermute | solution.py:14
  264.5 19.9 %collective-permute-start = (bf16[2,256,1024]{1,2,0:T(8,128)(2,1)}, bf16[2,256,1024]{1,2,0:T(8,128)(2,1)S(1)}, u32[]{:S(2)}, u32[]{:S(2)}) collective-permute-start(bf16[2,256,1024]{1,2,0:T(8,128)(2,1)} %get-tuple-element.511), channel_id=1, source_target_pairs={{0,1},{1,2},{2,3},{3,4},{4,5},{5,6},{6,7},{7,8},{8,9},{9,10},{10,1... | collective-permute-start | bytes 3145736 | tf_op jit(solution)/shard_map/while/body/eval_jaxpr/ppermute | solution.py:14
  286.8 5.8 conditional.3
  286.8 1.0 fusion.54
  288.7 3.9 fusion.4
  293.6 14.0 collective-permute-start
  311.1 19.9 %collective-permute-start = (bf16[2,256,1024]{1,2,0:T(8,128)(2,1)}, bf16[2,256,1024]{1,2,0:T(8,128)(2,1)S(1)}, u32[]{:S(2)}, u32[]{:S(2)}) collective-permute-start(bf16[2,256,1024]{1,2,0:T(8,128)(2,1)} %get-tuple-element.511), channel_id=1, source_target_pairs={{0,1},{1,2},{2,3},{3,4},{4,5},{5,6},{6,7},{7,8},{8,9},{9,10},{10,1... | collective-permute-start | bytes 3145736 | tf_op jit(solution)/shard_map/while/body/eval_jaxpr/ppermute | solution.py:14
  334.5 9.6 collective-permute-start
  345.8 3.1 collective-permute-done
  348.9 1.0 copy.64
  349.9 1.4 reduce_sum.89
  351.3 1.5 multiply_reduce_fusion.1
  352.9 3.0 multiply_reduce_fusion
  355.9 3.8 fusion.13
  360.8 4.8 convolution_multiply_fusion
  365.7 1302.4 %reduce-scatter.2.cloned.1.call-done = f32[8,1024]{1,0:T(8,128)} async-done(((f32[2048,1024]{1,0:T(8,128)}), f32[8,1024]{1,0:T(8,128)}) %reduce-scatter.2.cloned.1.call-update) | async-done | bytes 32784 | tf_op jit(solution)/shard_map/reduce_scatter | solution.py:121
  (105 shorter events, 28.2 us)
Async XLA Ops:
  7.2 345.7 %copy-start = (bf16[1024,1024]{1,0:T(8,128)(2,1)S(1)}, bf16[1024,1024]{1,0:T(8,128)(2,1)}, u32[]{:S(2)}) copy-start(bf16[1024,1024]{1,0:T(8,128)(2,1)} %param.15) | copy-start | bytes 6291460
  7.2 348.7 %all-gather.2.cloned.1.call-start = ((), (), s32[]{:S(2)}) async-start(), calls=%async_computation.1 | async-start | bytes 4456448 | tf_op jit(solution)/shard_map/all_gather | solution.py:104
  7.9 1660.2 %reduce-scatter.2.cloned.1.call-start = ((), (), s32[]{:S(2)}) async-start(), calls=%async_computation.2 | async-start | bytes 8421376 | tf_op jit(solution)/shard_map/reduce_scatter | solution.py:121
  16.6 1.9 copy-start.2
  16.6 2.9 copy-start.6
  16.7 3.1 copy-start.7
  30.7 14.4 collective-permute-start
  46.1 17.9 %collective-permute-start = (bf16[2,256,1024]{1,2,0:T(8,128)(2,1)}, bf16[2,256,1024]{1,2,0:T(8,128)(2,1)S(1)}, u32[]{:S(2)}, u32[]{:S(2)}) collective-permute-start(bf16[2,256,1024]{1,2,0:T(8,128)(2,1)} %get-tuple-element.511), channel_id=1, source_target_pairs={{0,1},{1,2},{2,3},{3,4},{4,5},{5,6},{6,7},{7,8},{8,9},{9,10},{10,1... | collective-permute-start | bytes 3145736 | tf_op jit(solution)/shard_map/while/body/eval_jaxpr/ppermute | solution.py:14
  70.8 14.4 collective-permute-start
  86.2 24.2 %collective-permute-start = (bf16[2,256,1024]{1,2,0:T(8,128)(2,1)}, bf16[2,256,1024]{1,2,0:T(8,128)(2,1)S(1)}, u32[]{:S(2)}, u32[]{:S(2)}) collective-permute-start(bf16[2,256,1024]{1,2,0:T(8,128)(2,1)} %get-tuple-element.511), channel_id=1, source_target_pairs={{0,1},{1,2},{2,3},{3,4},{4,5},{5,6},{6,7},{7,8},{8,9},{9,10},{10,1... | collective-permute-start | bytes 3145736 | tf_op jit(solution)/shard_map/while/body/eval_jaxpr/ppermute | solution.py:14
  111.4 22.4 %collective-permute-start = (bf16[2,256,1024]{1,2,0:T(8,128)(2,1)}, bf16[2,256,1024]{1,2,0:T(8,128)(2,1)S(1)}, u32[]{:S(2)}, u32[]{:S(2)}) collective-permute-start(bf16[2,256,1024]{1,2,0:T(8,128)(2,1)} %get-tuple-element.511), channel_id=1, source_target_pairs={{0,1},{1,2},{2,3},{3,4},{4,5},{5,6},{6,7},{7,8},{8,9},{9,10},{10,1... | collective-permute-start | bytes 3145736 | tf_op jit(solution)/shard_map/while/body/eval_jaxpr/ppermute | solution.py:14
  134.7 16.5 collective-permute-start
  152.2 28.2 %collective-permute-start = (bf16[2,256,1024]{1,2,0:T(8,128)(2,1)}, bf16[2,256,1024]{1,2,0:T(8,128)(2,1)S(1)}, u32[]{:S(2)}, u32[]{:S(2)}) collective-permute-start(bf16[2,256,1024]{1,2,0:T(8,128)(2,1)} %get-tuple-element.511), channel_id=1, source_target_pairs={{0,1},{1,2},{2,3},{3,4},{4,5},{5,6},{6,7},{7,8},{8,9},{9,10},{10,1... | collective-permute-start | bytes 3145736 | tf_op jit(solution)/shard_map/while/body/eval_jaxpr/ppermute | solution.py:14
  181.4 17.9 %collective-permute-start = (bf16[2,256,1024]{1,2,0:T(8,128)(2,1)}, bf16[2,256,1024]{1,2,0:T(8,128)(2,1)S(1)}, u32[]{:S(2)}, u32[]{:S(2)}) collective-permute-start(bf16[2,256,1024]{1,2,0:T(8,128)(2,1)} %get-tuple-element.511), channel_id=1, source_target_pairs={{0,1},{1,2},{2,3},{3,4},{4,5},{5,6},{6,7},{7,8},{8,9},{9,10},{10,1... | collective-permute-start | bytes 3145736 | tf_op jit(solution)/shard_map/while/body/eval_jaxpr/ppermute | solution.py:14
  200.2 22.4 %collective-permute-start = (bf16[2,256,1024]{1,2,0:T(8,128)(2,1)}, bf16[2,256,1024]{1,2,0:T(8,128)(2,1)S(1)}, u32[]{:S(2)}, u32[]{:S(2)}) collective-permute-start(bf16[2,256,1024]{1,2,0:T(8,128)(2,1)} %get-tuple-element.511), channel_id=1, source_target_pairs={{0,1},{1,2},{2,3},{3,4},{4,5},{5,6},{6,7},{7,8},{8,9},{9,10},{10,1... | collective-permute-start | bytes 3145736 | tf_op jit(solution)/shard_map/while/body/eval_jaxpr/ppermute | solution.py:14
  223.6 16.5 collective-permute-start
  241.1 22.4 %collective-permute-start = (bf16[2,256,1024]{1,2,0:T(8,128)(2,1)}, bf16[2,256,1024]{1,2,0:T(8,128)(2,1)S(1)}, u32[]{:S(2)}, u32[]{:S(2)}) collective-permute-start(bf16[2,256,1024]{1,2,0:T(8,128)(2,1)} %get-tuple-element.511), channel_id=1, source_target_pairs={{0,1},{1,2},{2,3},{3,4},{4,5},{5,6},{6,7},{7,8},{8,9},{9,10},{10,1... | collective-permute-start | bytes 3145736 | tf_op jit(solution)/shard_map/while/body/eval_jaxpr/ppermute | solution.py:14
  264.5 22.4 %collective-permute-start = (bf16[2,256,1024]{1,2,0:T(8,128)(2,1)}, bf16[2,256,1024]{1,2,0:T(8,128)(2,1)S(1)}, u32[]{:S(2)}, u32[]{:S(2)}) collective-permute-start(bf16[2,256,1024]{1,2,0:T(8,128)(2,1)} %get-tuple-element.511), channel_id=1, source_target_pairs={{0,1},{1,2},{2,3},{3,4},{4,5},{5,6},{6,7},{7,8},{8,9},{9,10},{10,1... | collective-permute-start | bytes 3145736 | tf_op jit(solution)/shard_map/while/body/eval_jaxpr/ppermute | solution.py:14
  293.6 16.5 collective-permute-start
  311.1 22.4 %collective-permute-start = (bf16[2,256,1024]{1,2,0:T(8,128)(2,1)}, bf16[2,256,1024]{1,2,0:T(8,128)(2,1)S(1)}, u32[]{:S(2)}, u32[]{:S(2)}) collective-permute-start(bf16[2,256,1024]{1,2,0:T(8,128)(2,1)} %get-tuple-element.511), channel_id=1, source_target_pairs={{0,1},{1,2},{2,3},{3,4},{4,5},{5,6},{6,7},{7,8},{8,9},{9,10},{10,1... | collective-permute-start | bytes 3145736 | tf_op jit(solution)/shard_map/while/body/eval_jaxpr/ppermute | solution.py:14
  334.5 14.4 collective-permute-start
  349.9 3.0 copy-start.1
  352.8 3.0 copy-start.4
  352.9 3.0 copy-start.5
  359.7 1.2 copy-start.3
Sparse Core Ops, SparseCore 0:
  10.6 110.4 all-gather.1
  365.8 1302.2 reduce-scatter.1
where the time goes:
time: 1700 us; the launch traced here: 1670 us
  waiting for transfers between devices  1350 us (79%)
  starting transfers between devices  223 us (13%)
  local copies, waits for them, and re-layouts  34.2 us (2%)
  matrix products  28.8 us (2%)
  loops' own time  19.2 us (1%)
    reduce_scatter x1, waiting for transfers between devices, shards(): lax.psum_scatter(local_grad, ('dp', 'ctx'), scatter_dimension=0, tiled=True)  1300 us
    ppermute x15, starting transfers between devices, passed_along(): return lax.ppermute(value, axis, pairs)  223 us
    ppermute x15, waiting for transfers between devices, passed_along(): return lax.ppermute(value, axis, pairs)  43.2 us
  transfers between devices with their start and end apart: 17, of which 16 were waited for; matrix products, arithmetic and copies ran while one was open for 4% of the time, Pallas kernels for 0%

commit v1 on v0

v1 whole, which is shorter than its diff:
```python
import functools
import math

import jax
import jax.numpy as jnp
from jax import lax
from jax.experimental import pallas as pl
from jax.experimental.pallas import tpu as pltpu
from jax.sharding import PartitionSpec as P

MESH = pl.DeviceIdType.MESH
F32 = jnp.float32
BF16 = jnp.bfloat16
ROWS, WIDTH, HEADS, HEAD = 256, 1024, 8, 128
SLOTS = 16
VMEM_LIMIT = 56 * 2**20


def place():
    dp = lax.axis_index("dp")
    ctx = lax.axis_index("ctx")
    return dp // 8, dp % 8, ctx // 8, (ctx // 2) % 4, ctx % 2


def device(xh, z, xl, y, c):
    return (xh * 8 + z, xl * 8 + y * 2 + c)


def remote(src, dst, send, recv, dev):
    return pltpu.make_async_remote_copy(
        src_ref=src, dst_ref=dst, send_sem=send, recv_sem=recv, device_id=dev, device_id_type=MESH
    )


def greet(others):
    barrier = pltpu.get_barrier_semaphore()
    for other in others:
        pl.semaphore_signal(barrier, inc=1, device_id=other, device_id_type=MESH)
    return barrier, len(others)


def silu(values):
    half = values * 0.5
    return half + half * jnp.tanh(half)


def norm(values):
    center = values - jnp.mean(values, axis=-1, keepdims=True)
    spread = jnp.mean(center * center, axis=-1, keepdims=True)
    return center * lax.rsqrt(spread + 1e-05)


def project_kernel(
    events, w_in, neg_in, gate_out, kv_all, q_all, neg_all,
    w_buf, normed, kv_st, q_st,
    w_sem, loc_sem, kv_ss, kv_rs, kv_fs, q_ss, q_rs, n_xs, n_ss, n_fs, n_rs,
):
    xh, z, xl, y, c = place()
    dp = lax.axis_index("dp")
    me = lax.axis_index("ctx")
    chip = me // 2
    sib = (dp, chip * 2 + 1 - c)
    z_up, z_down = lax.rem(z + 1, 8), lax.rem(z + 7, 8)
    up, down = device(xh, z_up, xl, y, c), device(xh, z_down, xl, y, c)
    across = device(1 - xh, z, xl, y, c)

    barrier, count = greet(
        [(dp, lax.rem(me + k, SLOTS)) for k in range(1, SLOTS)] + [up, down, across]
    )
    offsets = [3072, 1024, 3584, 1536, 2048, 2560, 0, 512]
    w_copies = [
        pltpu.make_async_copy(w_in.at[:, pl.ds(off, 512)], w_buf.at[i], w_sem.at[i])
        for i, off in enumerate(offsets)
    ]
    for copy in w_copies:
        copy.start()
    local = [
        pltpu.make_async_copy(neg_in.at[pl.ds(64 * k, 64)], neg_all.at[dp * 2 + k], loc_sem.at[k])
        for k in range(2)
    ]
    for copy in local:
        copy.start()
    normed[...] = norm(events[...].astype(F32)).astype(BF16)
    pl.semaphore_wait(barrier, count)

    own_neg = neg_in.at[pl.ds(pl.multiple_of(64 * c, 64), 64)]
    sends = []

    def neg_block(xh_, z_, c_):
        return (xh_ * 8 + z_) * 2 + c_

    def start(copy):
        copy.start()
        sends.append(copy)

    mine = neg_block(xh, z, c)
    start(remote(own_neg, neg_all.at[mine], n_xs, n_rs.at[mine], across))
    start(remote(own_neg, neg_all.at[mine], n_ss.at[0, 0], n_rs.at[mine], up))
    start(remote(own_neg, neg_all.at[mine], n_ss.at[1, 0], n_rs.at[mine], down))

    def block(i):
        w_copies[i].wait()
        return silu(jnp.dot(normed[...], w_buf[i], preferred_element_type=F32)).astype(BF16)

    def kv_send(h):
        return remote(kv_st.at[h], kv_all.at[me], kv_ss.at[h], kv_rs.at[me], (dp, 2 * h + c))

    def q_send(h, core):
        return remote(
            q_st.at[h, pl.ds(128 * core, 128)],
            q_all.at[me],
            q_ss.at[h, core],
            q_rs.at[me],
            (dp, 2 * h + core),
        )

    for half in range(2):
        for part in range(2):
            value = block(2 * half + part)
            for k in range(4):
                kv_st[4 * half + k, part] = value[:, 128 * k : 128 * (k + 1)]
        for k in range(4):
            h = 4 * half + k

            @pl.when(h != chip)
            def _(h=h):
                kv_send(h).start()

    kv_sib = remote(kv_st.at[chip], kv_all.at[me], kv_fs.at[me], kv_rs.at[me], sib)
    kv_sib.start()
    kv_own = pltpu.make_async_copy(kv_st.at[chip], kv_all.at[me], loc_sem.at[2])
    kv_own.start()
    for half in range(2):
        value = block(4 + half)
        for k in range(4):
            q_st[4 * half + k] = value[:, 128 * k : 128 * (k + 1)]
        for k in range(4):
            h = 4 * half + k

            @pl.when(h != chip)
            def _(h=h):
                q_send(h, 0).start()
                q_send(h, 1).start()

    rows_mine = pl.ds(pl.multiple_of(128 * c, 128), 128)
    rows_sib = pl.ds(pl.multiple_of(128 * (1 - c), 128), 128)
    q_sib = remote(q_st.at[chip, rows_sib], q_all.at[me], q_ss.at[8, 0], q_rs.at[me], sib)
    q_sib.start()
    q_own = pltpu.make_async_copy(q_st.at[chip, rows_mine], q_all.at[me], loc_sem.at[3])
    q_own.start()
    for half in range(2):
        gate_out[:, pl.ds(512 * half, 512)] = block(6 + half)

    def neg_arrived(index):
        remote(neg_all.at[index], neg_all.at[index], n_xs, n_rs.at[index], sib).wait_recv()

    def neg_pass(index, direction, count):
        target = up if direction == 0 else down
        start(remote(neg_all.at[index], neg_all.at[index], n_ss.at[direction, count], n_rs.at[index], target))

    def neg_sib(index):
        start(remote(neg_all.at[index], neg_all.at[index], n_fs.at[index // 2], n_rs.at[index], sib))

    index = neg_block(1 - xh, z, c)
    neg_arrived(index)
    neg_pass(index, 0, 1)
    neg_pass(index, 1, 1)
    neg_sib(index)
    for s in range(1, 5):
        for xh_ in range(2):
            if s < 4 or xh_ == 0:
                index = neg_block(xh_, lax.rem(z + 8 - s, 8), c)
                neg_arrived(index)
                if s < 3 or (s == 3 and xh_ == 0):
                    neg_pass(index, 0, 2 * s + xh_)
                neg_sib(index)
            if s < 4 or xh_ == 1:
                index = neg_block(xh_, lax.rem(z + s, 8), c)
                neg_arrived(index)
                if s < 3 or (s == 3 and xh_ == 1):
                    neg_pass(index, 1, 2 * s + xh_)
                neg_sib(index)
        if s == 3:
            for k in range(1, 8):
                src = lax.rem(chip + k, 8) * 2 + c
                ref = kv_all.at[src]
                remote(ref, ref, kv_fs.at[src], kv_rs.at[src], sib).wait_recv()
                start(remote(ref, ref, kv_fs.at[src], kv_rs.at[src], sib))

    for k in range(8):
        src = lax.rem(chip + k, 8) * 2 + 1 - c
        ref = kv_all.at[src]
        remote(ref, ref, kv_fs.at[src], kv_rs.at[src], sib).wait_recv()
    for k in range(1, SLOTS):
        src = lax.rem(me + k, SLOTS)
        remote(q_all.at[src], q_all.at[src], q_ss.at[0, 0], q_rs.at[src], sib).wait_recv()
    for xh_ in range(2):
        for k in range(8):
            z_ = lax.rem(z + k, 8)
            index = neg_block(xh_, z_, 1 - c)
            if k > 0:
                neg_arrived(index)
            else:

                @pl.when(xh_ != xh)
                def _(index=index):
                    neg_arrived(index)

    for copy in local + [kv_own, q_own]:
        copy.wait()
    for copy in sends + [kv_sib, q_sib]:
        copy.wait_send()
    for h in range(8):

        @pl.when(h != chip)
        def _(h=h):
            kv_send(h).wait_send()
            q_send(h, 0).wait_send()
            q_send(h, 1).wait_send()


def attend_kernel(lens, order, q, kv, out, slot_of):
    c = lax.axis_index("ctx") % 2
    for s in range(SLOTS):
        slot_of[order[0, s]] = s
    sizes = [lens[0, u] for u in range(4)]
    starts = [0, sizes[0], sizes[0] + sizes[1], sizes[0] + sizes[1] + sizes[2]]

    def pick(pos, values):
        got = jnp.where(pos >= starts[1], values[1], values[0])
        got = jnp.where(pos >= starts[2], values[2], got)
        return jnp.where(pos >= starts[3], values[3], got)

    row = lax.broadcasted_iota(jnp.int32, (ROWS, 1), 0)
    row = jnp.where(row < 128, row, row + 128) + 128 * c
    col = lax.broadcasted_iota(jnp.int32, (1, ROWS), 1)
    factor = 0.5 / math.sqrt(HEAD)

    def pair(p, carry):
        s0, s1 = slot_of[2 * p], slot_of[2 * p + 1]
        query = jnp.concatenate([q[s0], q[s1]], axis=0)
        q_pos = row + 512 * p
        q_start = pick(q_pos, starts)
        q_size = pick(q_pos, sizes).astype(F32)
        first = pick(512 * p + 128 * c, starts) // ROWS

        def step(kb, total):
            s = slot_of[kb]
            scores = lax.dot_general(
                query, kv[s, 0], (((1,), (1,)), ((), ())), preferred_element_type=F32
            )
            half = scores * factor
            weight = half + half * jnp.tanh(half)
            k_pos = col + kb * ROWS
            seen = (k_pos >= q_start) & (k_pos <= q_pos)
            weight = jnp.where(seen, weight, 0.0).astype(BF16)
            return total + jnp.dot(weight, kv[s, 1], preferred_element_type=F32)

        total = lax.fori_loop(first, 2 * p + 2, step, jnp.zeros((ROWS, HEAD), F32))
        total = (total / q_size).astype(BF16)
        out[s0] = total[:128]
        out[s1] = total[128:]
        return carry

    lax.fori_loop(0, SLOTS // 2, pair, 0)


def loss_kernel(
    att, gate_in, events_in, targets_in, target_ids, w_out_in, neg_in, neg_ids,
    loss_out, grad_out,
    heads, gate, events, targets, w_out, neg, mixed, user, user_sib, logits,
    p_own, p_send, p_recv, grad, ra1, rb1, sa, sb, ra2, rb2, tz, rz,
    loc_sem, a_ss, a_rs, u_sem, p_ss, p_rs, g_ss, g_rs, h_ss, h_rs, z_ss, z_rs,
):
    xh, z, xl, y, c = place()
    dp = lax.axis_index("dp")
    me = lax.axis_index("ctx")
    chip = me // 2
    sib = (dp, chip * 2 + 1 - c)
    xs = [(xh, 1 - xl), (1 - xh, xl), (1 - xh, 1 - xl)]
    x_peers = [device(a, z, b, y, c) for a, b in xs]
    ys = [lax.rem(y + k, 4) for k in range(1, 4)]
    y_peers = [device(xh, z, xl, b, c) for b in ys]
    zs = [lax.rem(z + k, 8) for k in range(1, 8)]
    z_peers = [device(xh, b, xl, y, c) for b in zs]

    barrier, count = greet(
        [(dp, lax.rem(me + k, SLOTS)) for k in range(1, SLOTS)] + x_peers[1:] + z_peers
    )
    loads = [
        pltpu.make_async_copy(src, dst, loc_sem.at[i])
        for i, (src, dst) in enumerate(
            [(gate_in, gate), (w_out_in, w_out), (events_in, events), (targets_in, targets), (neg_in, neg)]
        )
    ]
    for copy in loads:
        copy.start()
    pl.semaphore_wait(barrier, count)

    sends = []

    def start(copy):
        copy.start()
        sends.append(copy)

    for k in range(1, SLOTS):
        j = lax.rem(me + k, SLOTS)
        start(remote(att.at[j], heads.at[me], a_ss.at[k], a_rs.at[me], (dp, j)))
    heads[me] = att[me]

    ids = neg_ids[...].astype(F32)
    ids = jnp.concatenate([ids, jnp.zeros((112, 128), F32)], axis=0).T
    wanted = target_ids[...].astype(F32)

    for k in range(1, SLOTS):
        j = lax.rem(me + k, SLOTS)
        remote(heads.at[j], heads.at[j], a_ss.at[0], a_rs.at[j], sib).wait_recv()
    loads[0].wait()
    for core in range(2):
        rows = pl.ds(128 * core, 128)
        attended = jnp.concatenate([heads[2 * h + core] for h in range(HEADS)], axis=1)
        mixed[rows] = (norm(attended.astype(F32)) * gate[rows].astype(F32)).astype(BF16)
    for copy in loads[1:4]:
        copy.wait()
    vec = events[...].astype(F32) + jnp.dot(mixed[...], w_out[...], preferred_element_type=F32)
    user[...] = vec.astype(BF16)
    u_copy = remote(user, user_sib, u_sem.at[0], u_sem.at[1], sib)
    start(u_copy)
    scale = 1.0 / math.sqrt(WIDTH)
    pos_col = jnp.sum(user[...].astype(F32) * targets[...].astype(F32), axis=1, keepdims=True) * scale
    eye = lax.broadcasted_iota(jnp.int32, (ROWS, ROWS), 0) == lax.broadcasted_iota(
        jnp.int32, (ROWS, ROWS), 1
    )
    pos = jnp.sum(jnp.where(eye, pos_col, 0.0), axis=0, keepdims=True)

    loads[4].wait()
    top = pos
    for d in range(SLOTS):
        part = neg[pl.ds(2 * d, 2)].reshape(128, WIDTH)
        scores = (
            lax.dot_general(part, user[...], (((1,), (1,)), ((), ())), preferred_element_type=F32)
            * scale
        )
        allowed = ids[:, d : d + 1] != wanted
        scores = jnp.where(allowed, scores, -jnp.inf)
        top = jnp.maximum(top, jnp.max(scores, axis=0, keepdims=True))
        logits[d] = scores.reshape(8, 2, 8, ROWS)
    total = jnp.exp(pos - top)
    for d in range(SLOTS):
        weight = jnp.exp(logits[d] - top.reshape(1, 1, 1, ROWS))
        logits[d] = weight
        total = total + jnp.sum(weight.reshape(128, ROWS), axis=0, keepdims=True)
    loss_out[...] = top + jnp.log(total) - pos
    inverse = 1.0 / total
    for d in range(SLOTS):
        p_send[pl.ds(64 * d, 64)] = (logits[d, :, 1 - c].reshape(64, ROWS) * inverse).astype(BF16)
    p_copy = remote(p_send, p_recv, p_ss, p_rs, sib)
    start(p_copy)
    for d in range(SLOTS):
        p_own[pl.ds(64 * d, 64)] = (logits[d, :, c].reshape(64, ROWS) * inverse).astype(BF16)
    u_copy.wait_recv()
    p_copy.wait_recv()

    def grad_block(a, b):
        rows = pl.ds(pl.multiple_of((a * 8 + 4 * b) * 64, 256), 256)
        value = jnp.dot(p_own[rows], user[...], preferred_element_type=F32)
        value = value + jnp.dot(p_recv[rows], user_sib[...], preferred_element_type=F32)
        left = value[:, :512].reshape(4, 2, 4, 8, 512)
        right = value[:, 512:].reshape(4, 2, 4, 8, 512)
        grad[a, pl.ds(4 * b, 4)] = jnp.concatenate([left, right], axis=3).astype(BF16)

    def send_x(k):
        a, b = xs[k]
        start(remote(grad.at[a, pl.ds(0, 4), b], ra1.at[k], g_ss.at[k], g_rs.at[k], x_peers[k]))

    def send_y(k, a):
        start(
            remote(
                grad.at[a, pl.ds(4, 4), :, ys[k]],
                rb1.at[k, a],
                g_ss.at[3 + 2 * k + a],
                g_rs.at[3 + 2 * k + a],
                y_peers[k],
            )
        )

    grad_block(1 - xh, 0)
    send_x(1)
    send_x(2)
    grad_block(0, 1)
    for k in range(3):
        send_y(k, 0)
    grad_block(1, 1)
    for k in range(3):
        send_y(k, 1)
    grad_block(xh, 0)
    send_x(0)

    def up(ref):
        return ref[...].astype(F32)

    for k in range(3):
        remote(ra1.at[k], ra1.at[k], g_ss.at[k], g_rs.at[k], sib).wait_recv()
    sa[...] = (
        up(grad.at[xh, pl.ds(0, 4), xl]) + up(ra1.at[0]) + up(ra1.at[1]) + up(ra1.at[2])
    ).astype(BF16)
    for k in range(3):
        start(remote(sa.at[:, ys[k]], ra2.at[k], h_ss.at[k], h_rs.at[k], y_peers[k]))
    for k in range(3):
        for a in range(2):
            ref = rb1.at[k, a]
            remote(ref, ref, g_ss.at[0], g_rs.at[3 + 2 * k + a], sib).wait_recv()
    sb[...] = (
        up(grad.at[:, pl.ds(4, 4), :, y]) + up(rb1.at[0]) + up(rb1.at[1]) + up(rb1.at[2])
    ).astype(BF16)
    for k in range(3):
        a, b = xs[k]
        start(remote(sb.at[a, :, b], rb2.at[k], h_ss.at[3 + k], h_rs.at[3 + k], x_peers[k]))
    for k in range(3):
        remote(ra2.at[k], ra2.at[k], h_ss.at[0], h_rs.at[k], sib).wait_recv()
    tz[pl.ds(0, 4)] = (
        up(sa.at[:, y]) + up(ra2.at[0]) + up(ra2.at[1]) + up(ra2.at[2])
    ).astype(BF16)
    for k in range(3):
        remote(rb2.at[k], rb2.at[k], h_ss.at[0], h_rs.at[3 + k], sib).wait_recv()
    tz[pl.ds(4, 4)] = (
        up(sb.at[xh, :, xl]) + up(rb2.at[0]) + up(rb2.at[1]) + up(rb2.at[2])
    ).astype(BF16)
    for k in range(7):
        start(remote(tz.at[zs[k]], rz.at[k], z_ss.at[k], z_rs.at[k], z_peers[k]))
    for k in range(7):
        remote(rz.at[k], rz.at[k], z_ss.at[0], z_rs.at[k], sib).wait_recv()
    result = tz[z].astype(F32)
    for k in range(7):
        result = result + rz[k].astype(F32)
    result = result * scale
    grad_out[:, :512] = result[:8]
    grad_out[:, 512:] = result[8:]
    for copy in sends:
        copy.wait_send()


def shards(events, w_in, w_out, targets, target_ids, lengths, block_order, negatives, neg_ids):
    any_space = pl.BlockSpec(memory_space=pl.ANY)
    vmem = pl.BlockSpec(memory_space=pltpu.VMEM)
    smem = pl.BlockSpec(memory_space=pltpu.SMEM)
    dma = pltpu.SemaphoreType.DMA
    gate, kv_all, q_all, neg_all = pl.pallas_call(
        project_kernel,
        out_shape=(
            jax.ShapeDtypeStruct((ROWS, WIDTH), BF16),
            jax.ShapeDtypeStruct((SLOTS, 2, ROWS, HEAD), BF16),
            jax.ShapeDtypeStruct((SLOTS, 128, HEAD), BF16),
            jax.ShapeDtypeStruct((32, 64, WIDTH), BF16),
        ),
        in_specs=[vmem, any_space, any_space],
        out_specs=(vmem, any_space, any_space, any_space),
        scratch_shapes=[
            pltpu.VMEM((8, WIDTH, 512), BF16),
            pltpu.VMEM((ROWS, WIDTH), BF16),
            pltpu.VMEM((HEADS, 2, ROWS, HEAD), BF16),
            pltpu.VMEM((HEADS, ROWS, HEAD), BF16),
            dma((8,)),
            dma((4,)),
            dma((8,)),
            dma((SLOTS,)),
            dma((SLOTS,)),
            dma((9, 2)),
            dma((SLOTS,)),
            dma,
            dma((2, 8)),
            dma((SLOTS,)),
            dma((32,)),
        ],
        compiler_params=pltpu.CompilerParams(
            collective_id=1, has_side_effects=True, vmem_limit_bytes=VMEM_LIMIT
        ),
        name="project",
    )(events, w_in, negatives)

    att = pl.pallas_call(
        attend_kernel,
        out_shape=jax.ShapeDtypeStruct((SLOTS, 128, HEAD), BF16),
        in_specs=[smem, smem, vmem, vmem],
        out_specs=vmem,
        scratch_shapes=[pltpu.SMEM((SLOTS,), jnp.int32)],
        compiler_params=pltpu.CompilerParams(vmem_limit_bytes=VMEM_LIMIT),
        name="attend",
    )(lengths, block_order, q_all, kv_all)

    loss, grad = pl.pallas_call(
        loss_kernel,
        out_shape=(
            jax.ShapeDtypeStruct((1, ROWS), F32),
            jax.ShapeDtypeStruct((8, WIDTH), F32),
        ),
        in_specs=[vmem, any_space, any_space, any_space, vmem, any_space, any_space, vmem],
        out_specs=(vmem, vmem),
        scratch_shapes=[
            pltpu.VMEM((SLOTS, 128, HEAD), BF16),
            pltpu.VMEM((ROWS, WIDTH), BF16),
            pltpu.VMEM((ROWS, WIDTH), BF16),
            pltpu.VMEM((ROWS, WIDTH), BF16),
            pltpu.VMEM((WIDTH, WIDTH), BF16),
            pltpu.VMEM((32, 64, WIDTH), BF16),
            pltpu.VMEM((ROWS, WIDTH), BF16),
            pltpu.VMEM((ROWS, WIDTH), BF16),
            pltpu.VMEM((ROWS, WIDTH), BF16),
            pltpu.VMEM((SLOTS, 8, 2, 8, ROWS), F32),
            pltpu.VMEM((1024, ROWS), BF16),
            pltpu.VMEM((1024, ROWS), BF16),
            pltpu.VMEM((1024, ROWS), BF16),
            pltpu.VMEM((2, 8, 2, 4, 16, 512), BF16),
            pltpu.VMEM((3, 4, 4, 16, 512), BF16),
            pltpu.VMEM((3, 2, 4, 2, 16, 512), BF16),
            pltpu.VMEM((4, 4, 16, 512), BF16),
            pltpu.VMEM((2, 4, 2, 16, 512), BF16),
            pltpu.VMEM((3, 4, 16, 512), BF16),
            pltpu.VMEM((3, 4, 16, 512), BF16),
            pltpu.VMEM((8, 16, 512), BF16),
            pltpu.VMEM((7, 16, 512), BF16),
            dma((5,)),
            dma((SLOTS,)),
            dma((SLOTS,)),
            dma((2,)),
            dma,
            dma,
            dma((9,)),
            dma((9,)),
            dma((6,)),
            dma((6,)),
            dma((7,)),
            dma((7,)),
        ],
        compiler_params=pltpu.CompilerParams(
            collective_id=2, has_side_effects=True, vmem_limit_bytes=VMEM_LIMIT
        ),
        name="loss",
    )(
        att, gate, events, targets, target_ids.reshape(1, ROWS), w_out, neg_all,
        neg_ids.reshape(SLOTS, 128),
    )
    return (loss.reshape(ROWS), grad)


def solution(mesh):
    return jax.shard_map(
        shards,
        mesh=mesh,
        in_specs=(
            P(("dp", "ctx"), None),
            P(),
            P(),
            P(("dp", "ctx"), None),
            P(("dp", "ctx")),
            P("dp", None),
            P("dp", None),
            P("dp", None),
            P(),
        ),
        out_specs=(P(("dp", "ctx")), P(("dp", "ctx"), None)),
        check_vma=False,
    )
```

time: 1700 us -> 110 us (0.06); the launches traced: 1670 us -> 108 us
  waiting for transfers between devices: 1350 us -> 0 us
  starting transfers between devices: 223 us -> 0 us
  Pallas kernels: 0 us -> 105 us
  local copies, waits for them, and re-layouts: 34.2 us -> 2.6 us
  matrix products: 28.8 us -> 0 us
  loops' own time: 19.2 us -> 0 us
    reduce_scatter x1 -> x0, waiting for transfers between devices: 1300 us -> none  [shards(): lax.psum_scatter(local_grad, ('dp', 'ctx'), scatter_dimension=0, tiled=True)]
    ppermute x15 -> x0, starting transfers between devices: 223 us -> none  [passed_along(): return lax.ppermute(value, axis, pairs)]
    pallas_call x0 -> x3, Pallas kernels: none -> 105 us  [the longest x1 48.7 us: shards(): pl.pallas_call(loss_kernel, out_shape=(jax.ShapeDtypeStruct((1, ROWS), F3...]
    ppermute x15 -> x0, waiting for transfers between devices: 43.2 us -> none  [passed_along(): return lax.ppermute(value, axis, pairs)]
    dot_general x7 -> x0, matrix products: 28.8 us -> none  [the longest x3 11.1 us: add_tile(): jnp.einsum('hqk,khd->qhd', weights, value_part, preferred_element_type=jn...]
    another operation x16 -> x0, loops' own time: 19.2 us -> none  [the longest x1 17.9 us: shards(): lax.fori_loop(1, cycle_size, cycle_step, (running, key_value))]
  transfers between devices with their start and end apart: 17 -> 0, of which waited for: 16 -> 0; matrix products, arithmetic and copies ran while one was open for 4% -> 0% of each run, Pallas kernels for 0% -> 0%
where the time goes in v1:
time: 110 us; the launch traced here: 108 us
  Pallas kernels  105 us (95%)
  local copies, waits for them, and re-layouts  2.6 us (2%)
    pallas_call x1, Pallas kernels, shards(): pl.pallas_call(loss_kernel, out_shape=(jax.ShapeDtypeStruct((1, ROWS), F3...  48.7 us
    pallas_call x1, Pallas kernels, shards(): pl.pallas_call(project_kernel, out_shape=(jax.ShapeDtypeStruct((ROWS, WID...  39.4 us
    pallas_call x1, Pallas kernels, shards(): pl.pallas_call(attend_kernel, out_shape=jax.ShapeDtypeStruct((SLOTS, 128,...  17 us
    unnamed x2, local copies, waits for them, and re-layouts  2.6 us

profile of v1, /device:TPU:24, one launch (start us, length us, event | category | flops | bytes accessed | tf_op | source)
XLA Modules:
  0.0 108.3 jit_solution(3380886895359564701)
XLA Ops:
  0.6 39.4 %project.1 = (bf16[256,1024]{1,0:T(8,128)(2,1)}, bf16[16,2,256,128]{3,2,1,0:T(8,128)(2,1)}, bf16[16,128,128]{2,1,0:T(8,128)(2,1)}, bf16[32,64,1024]{2,1,0:T(8,128)(2,1)}) custom-call(bf16[256,1024]{1,0:T(8,128)(2,1)} %events_in.1, bf16[1024,4096]{1,0:T(8,128)(2,1)} %w_in.1, bf16[128,1024]{1,0:T(8,128)(2,1)} %neg_in.1), custom_call_target="tpu_custom_call" | custom-call | tf_op jit(solution)/shard_map/project/pallas_call | solution.py:448
  40.0 17.0 %attend.1.att = bf16[16,128,128]{2,1,0:T(8,128)(2,1)} custom-call(s32[1,4]{1,0:T(1,128)} %lens.1, s32[1,16]{1,0:T(1,128)} %order.1, bf16[16,128,128]{2,1,0:T(8,128)(2,1)} %get-tuple-element.8.q, bf16[16,2,256,128]{3,2,1,0:T(8,128)(2,1)} %get-tuple-element.9.kv), custom_call_target="tpu_custom_call" | custom-call | tf_op jit(solution)/shard_map/attend/pallas_call | solution.py:481
  57.0 48.7 %loss.1 = (f32[1,256]{1,0:T(1,128)}, f32[8,1024]{1,0:T(8,128)}) custom-call(bf16[16,128,128]{2,1,0:T(8,128)(2,1)} %attend.1.att, bf16[256,1024]{1,0:T(8,128)(2,1)} %get-tuple-element.10.gate_in, bf16[256,1024]{1,0:T(8,128)(2,1)} %events_in.1, bf16[256,1024]{1,0:T(8,128)(2,1)} %targets_in.1, s32[1,256]{1,0:T(1,128)} %bitcast.4, bf16[1024,1024]{1,0:T(8,128)(2,1)} %w_out_in.1, ...), custom_call_target="tpu_custom_call" | custom-call | tf_op jit(solution)/shard_map/loss/pallas_call | solution.py:491
  105.7 1.2 %copy.13 = f32[256]{0:T(256)} copy(f32[256]{0:T(256)} %bitcast.5) | data formatting | bytes 2048
  107.0 1.4 %copy.14 = f32[8,1024]{1,0:T(8,128)} copy(f32[8,1024]{1,0:T(8,128)} %get-tuple-element.17) | data formatting | bytes 65536

commit v2 on v1

v2 whole, which is shorter than its diff:
```python
import functools
import math

import jax
import jax.numpy as jnp
from jax import lax
from jax.experimental import pallas as pl
from jax.experimental.pallas import tpu as pltpu
from jax.sharding import PartitionSpec as P

MESH = pl.DeviceIdType.MESH
F32 = jnp.float32
BF16 = jnp.bfloat16
ROWS, WIDTH, HEADS, HEAD = 256, 1024, 8, 128
SLOTS = 16
VMEM_LIMIT = 56 * 2**20
RING = 2
PEERS = [(1, 2), (0, 2), (1, 1), (1, 3), (0, 1), (0, 3), (1, 0)]
TILES = 4


def place():
    dp = lax.axis_index("dp")
    ctx = lax.axis_index("ctx")
    return dp // 8, dp % 8, ctx // 8, (ctx // 2) % 4, ctx % 2


def device(xh, z, xl, y, c):
    return (xh * 8 + z, xl * 8 + y * 2 + c)


def remote(src, dst, send, recv, dev):
    return pltpu.make_async_remote_copy(
        src_ref=src, dst_ref=dst, send_sem=send, recv_sem=recv, device_id=dev, device_id_type=MESH
    )


def greet(others):
    barrier = pltpu.get_barrier_semaphore()
    for other in others:
        pl.semaphore_signal(barrier, inc=1, device_id=other, device_id_type=MESH)
    return barrier, len(others)


def silu(values):
    half = values * 0.5
    return half + half * jnp.tanh(half)


def norm(values):
    center = values - jnp.mean(values, axis=-1, keepdims=True)
    spread = jnp.mean(center * center, axis=-1, keepdims=True)
    return center * lax.rsqrt(spread + 1e-05)


def head_of(xl, y, peer):
    return (xl + peer[0]) % 2 * 4 + lax.rem(y + peer[1], 4)


def ring_blocks(xh, z, s):
    ups = [a * 8 + lax.rem(z + 8 - s, 8) for a in (xh, 1 - xh)]
    downs = [a * 8 + lax.rem(z + s, 8) for a in (xh, 1 - xh)]
    return ups, downs


def project_kernel(
    events, w_in, neg_in, gate_out, kv_all, q_all, neg_all,
    w_buf, normed, kv_st, q_st, neg_rows, neg_st,
    w_sem, loc_sem, kv_ss, kv_rs, kv_fs, q_ss, q_rs, n_xs, n_ss, n_rs,
):
    xh, z, xl, y, c = place()
    dp = lax.axis_index("dp")
    me = lax.axis_index("ctx")
    chip = me // 2
    sib = (dp, chip * 2 + 1 - c)
    z_up, z_down = lax.rem(z + 1, 8), lax.rem(z + 7, 8)
    up, down = device(xh, z_up, xl, y, c), device(xh, z_down, xl, y, c)
    across = device(1 - xh, z, xl, y, c)

    barrier, count = greet(
        [across, up, down] + [(dp, lax.rem(me + k, SLOTS)) for k in range(1, SLOTS)]
    )
    far = (1 - xl) * 512
    near = xl * 512
    offsets = [3072 + far, 1024 + far, 3072 + near, 1024 + near, 2048, 2560, 0, 512]
    w_copies = [
        pltpu.make_async_copy(
            w_in.at[:, pl.ds(pl.multiple_of(off, 512), 512)], w_buf.at[i], w_sem.at[i]
        )
        for i, off in enumerate(offsets)
    ]
    for copy in w_copies:
        copy.start()
    neg_rows[...] = neg_in[...].astype(F32).reshape(8, 2, 8, WIDTH)
    neg_st[...] = neg_rows[:, c].reshape(64, WIDTH).astype(BF16)
    neg_own = pltpu.make_async_copy(neg_st, neg_all.at[dp], loc_sem.at[0])
    neg_own.start()
    normed[...] = norm(events[...].astype(F32)).astype(BF16)
    pl.semaphore_wait(barrier, count)

    sends = []

    def start(copy):
        copy.start()
        sends.append(copy)

    start(remote(neg_st, neg_all.at[dp], n_xs, n_rs.at[dp], across))
    start(remote(neg_st, neg_all.at[dp], n_ss.at[0, 0], n_rs.at[dp], up))
    start(remote(neg_st, neg_all.at[dp], n_ss.at[1, 0], n_rs.at[dp], down))

    def ring(s, side):
        ups, downs = ring_blocks(xh, z, s)
        for direction, index in enumerate([ups[side], downs[side]]):
            if s == 0 and direction == 1:
                continue
            ref = neg_all.at[index]
            remote(ref, ref, n_xs, n_rs.at[index], sib).wait_recv()
        if s < RING:
            for direction, index in enumerate([ups[side], downs[side]]):
                ref = neg_all.at[index]
                target = up if direction == 0 else down
                start(remote(ref, ref, n_ss.at[direction, 2 * s + side], n_rs.at[index], target))

    def block(i):
        w_copies[i].wait()
        return silu(jnp.dot(normed[...], w_buf[i], preferred_element_type=F32)).astype(BF16)

    def kv_send(i):
        h = head_of(xl, y, PEERS[i])
        start(remote(kv_st.at[h], kv_all.at[me], kv_ss.at[i], kv_rs.at[me], (dp, 2 * h + c)))

    def q_send(i):
        h = head_of(xl, y, PEERS[i])
        for core in range(2):
            part = q_st.at[h, pl.ds(128 * core, 128)]
            start(remote(part, q_all.at[me], q_ss.at[i, core], q_rs.at[me], (dp, 2 * h + core)))

    for half, side in enumerate([1 - xl, xl]):
        for part in range(2):
            value = block(2 * half + part)
            for k in range(4):
                kv_st[4 * side + k, part] = value[:, 128 * k : 128 * (k + 1)]
        for i in range(7):
            if PEERS[i][0] == 1 - half:
                kv_send(i)
    ring(1, 0)
    kv_sib = remote(kv_st.at[chip], kv_all.at[me], kv_fs.at[me], kv_rs.at[me], sib)
    kv_sib.start()
    kv_own = pltpu.make_async_copy(kv_st.at[chip], kv_all.at[me], loc_sem.at[1])
    kv_own.start()
    for half in range(2):
        value = block(4 + half)
        for k in range(4):
            q_st[4 * half + k] = value[:, 128 * k : 128 * (k + 1)]
    ring(0, 1)
    for i in range(7):
        q_send(i)

    rows_mine = pl.ds(pl.multiple_of(128 * c, 128), 128)
    rows_sib = pl.ds(pl.multiple_of(128 * (1 - c), 128), 128)
    q_sib = remote(q_st.at[chip, rows_sib], q_all.at[me], q_ss.at[7, 0], q_rs.at[me], sib)
    q_sib.start()
    q_own = pltpu.make_async_copy(q_st.at[chip, rows_mine], q_all.at[me], loc_sem.at[2])
    q_own.start()
    gate_out[:, pl.ds(0, 512)] = block(6)
    gate_out[:, pl.ds(512, 512)] = block(7)
    ring(1, 1)
    for s in range(2, RING + 1):
        ring(s, 0)
        ring(s, 1)

    for i in range(7):
        src = head_of(xl, y, PEERS[i]) * 2 + c
        ref = kv_all.at[src]
        remote(ref, ref, kv_fs.at[src], kv_rs.at[src], sib).wait_recv()
        start(remote(ref, ref, kv_fs.at[src], kv_rs.at[src], sib))
    for k in range(1, SLOTS):
        src = lax.rem(me + k, SLOTS)
        remote(q_all.at[src], q_all.at[src], q_ss.at[0, 0], q_rs.at[src], sib).wait_recv()
    for k in range(8):
        src = lax.rem(chip + k, 8) * 2 + 1 - c
        ref = kv_all.at[src]
        remote(ref, ref, kv_fs.at[src], kv_rs.at[src], sib).wait_recv()
    for copy in [neg_own, kv_own, q_own]:
        copy.wait()
    for copy in sends + [kv_sib, q_sib]:
        copy.wait_send()


def attend_kernel(lens, order, q, kv, out, slot_of, work, total, q_start, query, key):
    c = lax.axis_index("ctx") % 2
    for s in range(SLOTS):
        slot_of[order[0, s]] = s
    sizes = [lens[0, u] for u in range(4)]
    starts = [0, sizes[0], sizes[0] + sizes[1], sizes[0] + sizes[1] + sizes[2]]

    def pick(pos, values):
        got = jnp.where(pos >= starts[1], values[1], values[0])
        got = jnp.where(pos >= starts[2], values[2], got)
        return jnp.where(pos >= starts[3], values[3], got)

    row = lax.broadcasted_iota(jnp.int32, (ROWS, HEAD), 0)
    row = jnp.where(row < 128, row, row + 128) + 128 * c
    col = lax.broadcasted_iota(jnp.int32, (ROWS, HEAD), 1)
    factor = 0.5 / math.sqrt(HEAD)

    count = 0
    for p in range(SLOTS // 2):

        def put(kb, n, p=p):
            work[n] = p * SLOTS + kb
            return n + 1

        first = pick(512 * p + 128 * c, starts) // ROWS
        count = lax.fori_loop(first, 2 * p + 2, put, count)
    for u in range(TILES):
        work[count + u] = SLOTS - 1

    for p in range(SLOTS // 2):
        q_start[p] = pick(row + 512 * p, starts)
        query[p, :128] = q[slot_of[2 * p]]
        query[p, 128:] = q[slot_of[2 * p + 1]]
    for s in range(SLOTS):
        key[s] = kv[s, 0].T
    total[...] = jnp.zeros_like(total)

    def step(i, carry):
        found = []
        for u in range(TILES):
            item = work[TILES * i + u]
            p, kb = item // SLOTS, item % SLOTS
            s = slot_of[kb]
            half = jnp.dot(query[p], key[s], preferred_element_type=F32) * factor
            weight = half + half * jnp.tanh(half)
            q_pos = row + 512 * p
            low = q_start[p]
            parts = []
            for j in range(2):
                k_pos = col + (kb * ROWS + HEAD * j)
                seen = (k_pos >= low) & (k_pos <= q_pos)
                part = weight[:, HEAD * j : HEAD * (j + 1)]
                parts.append(jnp.where(seen, part, 0.0).astype(BF16))
            weight = jnp.concatenate(parts, axis=1)
            found.append((p, jnp.dot(weight, kv[s, 1], preferred_element_type=F32)))
        for p, value in found:
            total[p] += value
        return carry

    lax.fori_loop(0, (count + TILES - 1) // TILES, step, 0)
    for p in range(SLOTS // 2):
        size = pick(row + 512 * p, sizes).astype(F32)
        value = (total[p] / size).astype(BF16)
        out[slot_of[2 * p]] = value[:128]
        out[slot_of[2 * p + 1]] = value[128:]


def loss_kernel(
    att, gate_in, events_in, targets_in, target_ids, w_out_in, neg_in, neg_ids,
    loss_out, grad_out,
    heads, gate, events, targets, w_out, neg, mixed, users, wanted, stats, stats_sib,
    logits, prob, grad, ra1, rb1, sa, sb, ra2, rb2, tz, rz,
    loc_sem, neg_sem, n_ss, n_rs, a_ss, a_rs, u_sem, t_sem, s_sem,
    g_ss, g_rs, h_ss, h_rs, z_ss, z_rs,
):
    xh, z, xl, y, c = place()
    dp = lax.axis_index("dp")
    me = lax.axis_index("ctx")
    chip = me // 2
    sib = (dp, chip * 2 + 1 - c)
    xs = [(xh, 1 - xl), (1 - xh, xl), (1 - xh, 1 - xl)]
    x_peers = [device(a, z, b, y, c) for a, b in xs]
    ys = [lax.rem(y + k, 4) for k in range(1, 4)]
    y_peers = [device(xh, z, xl, b, c) for b in ys]
    zs = [lax.rem(z + k, 8) for k in range(1, 8)]
    z_peers = [device(xh, b, xl, y, c) for b in zs]

    barrier, count = greet(
        [(dp, lax.rem(me + k, SLOTS)) for k in range(1, SLOTS)] + z_peers + x_peers[1:]
    )
    loads = [
        pltpu.make_async_copy(src, dst, loc_sem.at[i])
        for i, (src, dst) in enumerate(
            [(gate_in, gate), (w_out_in, w_out), (events_in, events), (targets_in, targets)]
        )
    ]
    held = [xh * 8 + z, (1 - xh) * 8 + z]
    for s in range(1, RING + 1):
        ups, downs = ring_blocks(xh, z, s)
        held += ups + downs
    loads += [
        pltpu.make_async_copy(neg_in.at[index], neg.at[index], neg_sem.at[i])
        for i, index in enumerate(held)
    ]
    for copy in loads:
        copy.start()
    pl.semaphore_wait(barrier, count)

    sends = []

    def start(copy):
        copy.start()
        sends.append(copy)

    def ring_send(source, index, direction, i):
        target = z_peers[0] if direction == 0 else z_peers[6]
        start(remote(source, neg.at[index], n_ss.at[direction, i], n_rs.at[index], target))

    def ring_wait(index):
        remote(neg.at[index], neg.at[index], n_ss.at[0, 0], n_rs.at[index], sib).wait_recv()

    ups = [lax.rem(z + 8 - s, 8) for s in range(5)]
    downs = [lax.rem(z + s, 8) for s in range(5)]
    if RING == 2:
        for i in range(2):
            index = 8 * i + ups[2]
            ring_send(neg_in.at[index], index, 0, i)
            index = 8 * i + downs[2]
            ring_send(neg_in.at[index], index, 1, i)
    else:
        ring_send(neg_in.at[ups[3]], ups[3], 0, 0)
        ring_send(neg_in.at[8 + downs[3]], 8 + downs[3], 1, 0)

    for i in range(7):
        h = head_of(xl, y, PEERS[i])
        for core in range(2):
            j = 2 * h + core
            start(remote(att.at[j], heads.at[me], a_ss.at[2 * i + core], a_rs.at[me], (dp, j)))
    start(remote(att.at[chip * 2 + 1 - c], heads.at[me], a_ss.at[14], a_rs.at[me], sib))
    heads[me] = att[me]

    wanted[0] = target_ids[...].astype(F32)
    t_copy = remote(wanted.at[0], wanted.at[1], t_sem.at[0], t_sem.at[1], sib)
    start(t_copy)
    ids = neg_ids[...].astype(F32)
    ids = jnp.concatenate([ids, jnp.zeros((112, 128), F32)], axis=0).T.reshape(8, 2, 8, 128)
    ids = jnp.where(c == 0, ids[:, 0], ids[:, 1]).reshape(64, 128)

    if RING == 2:
        for i in range(2):
            ring_wait(8 * i + ups[3])
            ring_wait(8 * i + downs[3])
        ring_send(neg.at[ups[3]], ups[3], 0, 2)
        ring_send(neg.at[8 + downs[3]], 8 + downs[3], 1, 2)

    for k in range(1, SLOTS):
        j = lax.rem(me + k, SLOTS)
        remote(heads.at[j], heads.at[j], a_ss.at[0], a_rs.at[j], sib).wait_recv()
    loads[0].wait()
    for core in range(2):
        rows = pl.ds(128 * core, 128)
        attended = jnp.concatenate([heads[2 * h + core] for h in range(HEADS)], axis=1)
        mixed[rows] = (norm(attended.astype(F32)) * gate[rows].astype(F32)).astype(BF16)
    for copy in loads[1:4]:
        copy.wait()
    vec = events[...].astype(F32) + jnp.dot(mixed[...], w_out[...], preferred_element_type=F32)
    users[0] = vec.astype(BF16)
    u_copy = remote(users.at[0], users.at[1], u_sem.at[0], u_sem.at[1], sib)
    start(u_copy)
    scale = 1.0 / math.sqrt(WIDTH)
    pos_col = jnp.sum(users[0].astype(F32) * targets[...].astype(F32), axis=1, keepdims=True) * scale
    eye = lax.broadcasted_iota(jnp.int32, (ROWS, ROWS), 0) == lax.broadcasted_iota(
        jnp.int32, (ROWS, ROWS), 1
    )
    pos = jnp.sum(jnp.where(eye, pos_col, 0.0), axis=0, keepdims=True)

    for copy in loads[4:]:
        copy.wait()
    ring_wait(ups[4])
    ring_wait(8 + downs[4])

    def score(side, top):
        for d in range(0, SLOTS, 4):
            part = neg[pl.ds(d, 4)].reshape(ROWS, WIDTH)
            scores = (
                lax.dot_general(
                    part, users[side], (((1,), (1,)), ((), ())), preferred_element_type=F32
                )
                * scale
            )
            id_col = jnp.concatenate([ids[:, d + i : d + i + 1] for i in range(4)], axis=0)
            scores = jnp.where(id_col != wanted[side], scores, -jnp.inf)
            top = jnp.maximum(top, jnp.max(scores, axis=0, keepdims=True))
            logits[side, pl.ds(64 * d, ROWS)] = scores
        return top

    def weigh(side, top, total):
        for d in range(4):
            rows = pl.ds(ROWS * d, ROWS)
            weight = jnp.exp(logits[side, rows] - top)
            logits[side, rows] = weight
            total = total + jnp.sum(weight, axis=0, keepdims=True)
        stats[2 * side : 2 * side + 1] = top
        stats[2 * side + 1 : 2 * side + 2] = total

    top = score(0, pos)
    weigh(0, top, jnp.exp(pos - top))
    t_copy.wait_recv()
    u_copy.wait_recv()
    top = score(1, jnp.full((1, ROWS), -1e30, F32))
    weigh(1, top, jnp.zeros((1, ROWS), F32))
    s_copy = remote(stats, stats_sib, s_sem.at[0], s_sem.at[1], sib)
    start(s_copy)
    s_copy.wait_recv()
    for side in range(2):
        near_top, near_sum = stats[2 * side : 2 * side + 1], stats[2 * side + 1 : 2 * side + 2]
        far = 2 * (1 - side)
        far_top, far_sum = stats_sib[far : far + 1], stats_sib[far + 1 : far + 2]
        top = jnp.maximum(near_top, far_top)
        near, far = jnp.exp(near_top - top), jnp.exp(far_top - top)
        total = near_sum * near + far_sum * far
        if side == 0:
            loss_out[...] = top + jnp.log(total) - pos
        factor = near / total
        for d in range(4):
            rows = pl.ds(ROWS * d, ROWS)
            prob[rows, pl.ds(ROWS * side, ROWS)] = (logits[side, rows] * factor).astype(BF16)

    def grad_block(n, a, b):
        rows = pl.ds(pl.multiple_of((a * 8 + 4 * b) * 64, 256), 256)
        sides = []
        for k in range(2):
            value = jnp.dot(
                prob[rows],
                users[:, :, pl.ds(512 * k + 256 * n, 256)].reshape(2 * ROWS, 256),
                preferred_element_type=F32,
            )
            sides.append(value.reshape(4, 2, 4, 8, 256))
        grad[n, a, pl.ds(4 * b, 4)] = jnp.concatenate(sides, axis=3).astype(BF16)

    def send_x(n, k):
        a, b = xs[k]
        start(
            remote(
                grad.at[n, a, pl.ds(0, 4), b], ra1.at[n, k], g_ss.at[n, k], g_rs.at[n, k], x_peers[k]
            )
        )

    def send_y(n, k, a):
        i = 3 + 2 * k + a
        start(
            remote(
                grad.at[n, a, pl.ds(4, 4), :, ys[k]],
                rb1.at[n, k, a],
                g_ss.at[n, i],
                g_rs.at[n, i],
                y_peers[k],
            )
        )

    for n in range(2):
        grad_block(n, 1 - xh, 0)
        send_x(n, 2)
        send_x(n, 1)
        grad_block(n, 0, 1)
        for k in (1, 0, 2):
            send_y(n, k, 0)
        grad_block(n, xh, 0)
        send_x(n, 0)
        grad_block(n, 1, 1)
        for k in (1, 0, 2):
            send_y(n, k, 1)

    def up(ref):
        return ref[...].astype(F32)

    for n in range(2):
        for k in range(3):
            remote(ra1.at[n, k], ra1.at[n, k], g_ss.at[n, k], g_rs.at[n, k], sib).wait_recv()
        sa[n] = (
            up(grad.at[n, xh, pl.ds(0, 4), xl]) + up(ra1.at[n, 0]) + up(ra1.at[n, 1]) + up(ra1.at[n, 2])
        ).astype(BF16)
        for k in (1, 0, 2):
            start(
                remote(sa.at[n, :, ys[k]], ra2.at[n, k], h_ss.at[n, k], h_rs.at[n, k], y_peers[k])
            )
        for k in range(3):
            for a in range(2):
                ref = rb1.at[n, k, a]
                remote(ref, ref, g_ss.at[n, 0], g_rs.at[n, 3 + 2 * k + a], sib).wait_recv()
        sb[n] = (
            up(grad.at[n, :, pl.ds(4, 4), :, y])
            + up(rb1.at[n, 0])
            + up(rb1.at[n, 1])
            + up(rb1.at[n, 2])
        ).astype(BF16)
        for k in (2, 1, 0):
            a, b = xs[k]
            start(
                remote(
                    sb.at[n, a, :, b], rb2.at[n, k], h_ss.at[n, 3 + k], h_rs.at[n, 3 + k], x_peers[k]
                )
            )
    for n in range(2):
        for k in range(3):
            remote(ra2.at[n, k], ra2.at[n, k], h_ss.at[n, 0], h_rs.at[n, k], sib).wait_recv()
        tz[n, pl.ds(0, 4)] = (
            up(sa.at[n, :, y]) + up(ra2.at[n, 0]) + up(ra2.at[n, 1]) + up(ra2.at[n, 2])
        ).astype(BF16)
        for k in range(3):
            remote(rb2.at[n, k], rb2.at[n, k], h_ss.at[n, 0], h_rs.at[n, 3 + k], sib).wait_recv()
        tz[n, pl.ds(4, 4)] = (
            up(sb.at[n, xh, :, xl]) + up(rb2.at[n, 0]) + up(rb2.at[n, 1]) + up(rb2.at[n, 2])
        ).astype(BF16)
        for k in (3, 2, 4, 1, 5, 0, 6):
            start(remote(tz.at[n, zs[k]], rz.at[n, k], z_ss.at[n, k], z_rs.at[n, k], z_peers[k]))
    for n in range(2):
        result = tz[n, z].astype(F32)
        for k in range(7):
            remote(rz.at[n, k], rz.at[n, k], z_ss.at[n, 0], z_rs.at[n, k], sib).wait_recv()
            result = result + rz[n, k].astype(F32)
        result = result * scale
        grad_out[:, pl.ds(256 * n, 256)] = result[:8]
        grad_out[:, pl.ds(512 + 256 * n, 256)] = result[8:]
    for copy in sends:
        copy.wait_send()


def shards(events, w_in, w_out, targets, target_ids, lengths, block_order, negatives, neg_ids):
    any_space = pl.BlockSpec(memory_space=pl.ANY)
    vmem = pl.BlockSpec(memory_space=pltpu.VMEM)
    smem = pl.BlockSpec(memory_space=pltpu.SMEM)
    dma = pltpu.SemaphoreType.DMA
    gate, kv_all, q_all, neg_all = pl.pallas_call(
        project_kernel,
        out_shape=(
            jax.ShapeDtypeStruct((ROWS, WIDTH), BF16),
            jax.ShapeDtypeStruct((SLOTS, 2, ROWS, HEAD), BF16),
            jax.ShapeDtypeStruct((SLOTS, 128, HEAD), BF16),
            jax.ShapeDtypeStruct((SLOTS, 64, WIDTH), BF16),
        ),
        in_specs=[vmem, any_space, vmem],
        out_specs=(vmem, any_space, any_space, any_space),
        scratch_shapes=[
            pltpu.VMEM((8, WIDTH, 512), BF16),
            pltpu.VMEM((ROWS, WIDTH), BF16),
            pltpu.VMEM((HEADS, 2, ROWS, HEAD), BF16),
            pltpu.VMEM((HEADS, ROWS, HEAD), BF16),
            pltpu.VMEM((8, 2, 8, WIDTH), F32),
            pltpu.VMEM((64, WIDTH), BF16),
            dma((8,)),
            dma((3,)),
            dma((8,)),
            dma((SLOTS,)),
            dma((SLOTS,)),
            dma((8, 2)),
            dma((SLOTS,)),
            dma,
            dma((2, 2 * RING)),
            dma((SLOTS,)),
        ],
        compiler_params=pltpu.CompilerParams(
            collective_id=1, has_side_effects=True, vmem_limit_bytes=VMEM_LIMIT
        ),
        name="project",
    )(events, w_in, negatives)

    att = pl.pallas_call(
        attend_kernel,
        out_shape=jax.ShapeDtypeStruct((SLOTS, 128, HEAD), BF16),
        in_specs=[smem, smem, vmem, vmem],
        out_specs=vmem,
        scratch_shapes=[
            pltpu.SMEM((SLOTS,), jnp.int32),
            pltpu.SMEM((96,), jnp.int32),
            pltpu.VMEM((SLOTS // 2, ROWS, HEAD), F32),
            pltpu.VMEM((SLOTS // 2, ROWS, HEAD), jnp.int32),
            pltpu.VMEM((SLOTS // 2, ROWS, HEAD), BF16),
            pltpu.VMEM((SLOTS, HEAD, ROWS), BF16),
        ],
        compiler_params=pltpu.CompilerParams(vmem_limit_bytes=VMEM_LIMIT),
        name="attend",
    )(lengths, block_order, q_all, kv_all)

    loss, grad = pl.pallas_call(
        loss_kernel,
        out_shape=(
            jax.ShapeDtypeStruct((1, ROWS), F32),
            jax.ShapeDtypeStruct((8, WIDTH), F32),
        ),
        in_specs=[vmem, any_space, any_space, any_space, vmem, any_space, any_space, vmem],
        out_specs=(vmem, vmem),
        scratch_shapes=[
            pltpu.VMEM((SLOTS, 128, HEAD), BF16),
            pltpu.VMEM((ROWS, WIDTH), BF16),
            pltpu.VMEM((ROWS, WIDTH), BF16),
            pltpu.VMEM((ROWS, WIDTH), BF16),
            pltpu.VMEM((WIDTH, WIDTH), BF16),
            pltpu.VMEM((SLOTS, 64, WIDTH), BF16),
            pltpu.VMEM((ROWS, WIDTH), BF16),
            pltpu.VMEM((2, ROWS, WIDTH), BF16),
            pltpu.VMEM((2, 1, ROWS), F32),
            pltpu.VMEM((8, ROWS), F32),
            pltpu.VMEM((8, ROWS), F32),
            pltpu.VMEM((2, 1024, ROWS), F32),
            pltpu.VMEM((1024, 2 * ROWS), BF16),
            pltpu.VMEM((2, 2, 8, 2, 4, 16, 256), BF16),
            pltpu.VMEM((2, 3, 4, 4, 16, 256), BF16),
            pltpu.VMEM((2, 3, 2, 4, 2, 16, 256), BF16),
            pltpu.VMEM((2, 4, 4, 16, 256), BF16),
            pltpu.VMEM((2, 2, 4, 2, 16, 256), BF16),
            pltpu.VMEM((2, 3, 4, 16, 256), BF16),
            pltpu.VMEM((2, 3, 4, 16, 256), BF16),
            pltpu.VMEM((2, 8, 16, 256), BF16),
            pltpu.VMEM((2, 7, 16, 256), BF16),
            dma((4,)),
            dma((2 + 4 * RING,)),
            dma((2, 3)),
            dma((SLOTS,)),
            dma((15,)),
            dma((SLOTS,)),
            dma((2,)),
            dma((2,)),
            dma((2,)),
            dma((2, 9)),
            dma((2, 9)),
            dma((2, 6)),
            dma((2, 6)),
            dma((2, 7)),
            dma((2, 7)),
        ],
        compiler_params=pltpu.CompilerParams(
            collective_id=2, has_side_effects=True, vmem_limit_bytes=VMEM_LIMIT
        ),
        name="loss",
    )(
        att, gate, events, targets, target_ids.reshape(1, ROWS), w_out, neg_all,
        neg_ids.reshape(SLOTS, 128),
    )
    return (loss.reshape(ROWS), grad)


def solution(mesh):
    return jax.shard_map(
        shards,
        mesh=mesh,
        in_specs=(
            P(("dp", "ctx"), None),
            P(),
            P(),
            P(("dp", "ctx"), None),
            P(("dp", "ctx")),
            P("dp", None),
            P("dp", None),
            P("dp", None),
            P(),
        ),
        out_specs=(P(("dp", "ctx")), P(("dp", "ctx"), None)),
        check_vma=False,
    )
```

time: 110 us -> 91.5 us (0.83)
  Pallas kernels: 105 us -> 87.2 us
    pallas_call x1, Pallas kernels: 39.4 us -> 30.3 us  [shards(): pl.pallas_call(project_kernel, out_shape=(jax.ShapeDtypeStruct((ROWS, WID...]
    pallas_call x1, Pallas kernels: 17 us -> 11.4 us  [shards(): pl.pallas_call(attend_kernel, out_shape=jax.ShapeDtypeStruct((SLOTS, 128,...]
    pallas_call x1, Pallas kernels: 48.7 us -> 45.5 us  [shards(): pl.pallas_call(loss_kernel, out_shape=(jax.ShapeDtypeStruct((1, ROWS), F3...]
where the time goes in v2:
time: 91.5 us; the launch traced here: 90.4 us
  Pallas kernels  87.2 us (95%)
  local copies, waits for them, and re-layouts  2.59 us (3%)
    pallas_call x1, Pallas kernels, shards(): pl.pallas_call(loss_kernel, out_shape=(jax.ShapeDtypeStruct((1, ROWS), F3...  45.5 us
    pallas_call x1, Pallas kernels, shards(): pl.pallas_call(project_kernel, out_shape=(jax.ShapeDtypeStruct((ROWS, WID...  30.3 us
    pallas_call x1, Pallas kernels, shards(): pl.pallas_call(attend_kernel, out_shape=jax.ShapeDtypeStruct((SLOTS, 128,...  11.4 us
    unnamed x2, local copies, waits for them, and re-layouts  2.59 us

profile of v2, /device:TPU:24, one launch (start us, length us, event | category | flops | bytes accessed | tf_op | source)
XLA Modules:
  0.0 90.4 jit_solution(2325623321592189038)
XLA Ops:
  0.6 30.3 %project.1 = (bf16[256,1024]{1,0:T(8,128)(2,1)}, bf16[16,2,256,128]{3,2,1,0:T(8,128)(2,1)}, bf16[16,128,128]{2,1,0:T(8,128)(2,1)}, bf16[16,64,1024]{2,1,0:T(8,128)(2,1)}) custom-call(bf16[256,1024]{1,0:T(8,128)(2,1)} %events_in.1, bf16[1024,4096]{1,0:T(8,128)(2,1)} %w_in.1, bf16[128,1024]{1,0:T(8,128)(2,1)} %neg_in.1), custom_call_target="tpu_custom_call" | custom-call | tf_op jit(solution)/shard_map/project/pallas_call | solution.py:523
  30.9 11.4 %attend.1.att = bf16[16,128,128]{2,1,0:T(8,128)(2,1)} custom-call(s32[1,4]{1,0:T(1,128)} %lens.1, s32[1,16]{1,0:T(1,128)} %order.1, bf16[16,128,128]{2,1,0:T(8,128)(2,1)} %get-tuple-element.8.q, bf16[16,2,256,128]{3,2,1,0:T(8,128)(2,1)} %get-tuple-element.9.kv), custom_call_target="tpu_custom_call" | custom-call | tf_op jit(solution)/shard_map/attend/pallas_call | solution.py:557
  42.3 45.5 %loss.1 = (f32[1,256]{1,0:T(1,128)}, f32[8,1024]{1,0:T(8,128)}) custom-call(bf16[16,128,128]{2,1,0:T(8,128)(2,1)} %attend.1.att, bf16[256,1024]{1,0:T(8,128)(2,1)} %get-tuple-element.10.gate_in, bf16[256,1024]{1,0:T(8,128)(2,1)} %events_in.1, bf16[256,1024]{1,0:T(8,128)(2,1)} %targets_in.1, s32[1,256]{1,0:T(1,128)} %bitcast.5, bf16[1024,1024]{1,0:T(8,128)(2,1)} %w_out_in.1, ...), custom_call_target="tpu_custom_call" | custom-call | tf_op jit(solution)/shard_map/loss/pallas_call | solution.py:574
  87.8 1.2 %copy.13 = f32[256]{0:T(256)} copy(f32[256]{0:T(256)} %bitcast.4) | data formatting | bytes 2048
  89.0 1.4 %copy.14 = f32[8,1024]{1,0:T(8,128)} copy(f32[8,1024]{1,0:T(8,128)} %get-tuple-element.17) | data formatting | bytes 65536

commit v3 on v2

v3 whole, which is shorter than its diff:
```python
import functools
import math

import jax
import jax.numpy as jnp
from jax import lax
from jax.experimental import pallas as pl
from jax.experimental.pallas import tpu as pltpu
from jax.sharding import PartitionSpec as P

MESH = pl.DeviceIdType.MESH
F32 = jnp.float32
BF16 = jnp.bfloat16
ROWS, WIDTH, HEADS, HEAD = 256, 1024, 8, 128
SLOTS = 16
VMEM_LIMIT = 56 * 2**20
PEERS = [(1, 0), (0, 1), (1, 1), (0, 3), (1, 3), (0, 2), (1, 2)]


def place():
    dp = lax.axis_index("dp")
    ctx = lax.axis_index("ctx")
    return dp // 8, dp % 8, ctx // 8, (ctx // 2) % 4, ctx % 2


def device(xh, z, xl, y, c):
    return (xh * 8 + z, xl * 8 + y * 2 + c)


def remote(src, dst, send, recv, dev):
    return pltpu.make_async_remote_copy(
        src_ref=src, dst_ref=dst, send_sem=send, recv_sem=recv, device_id=dev, device_id_type=MESH
    )


def greet(others):
    barrier = pltpu.get_barrier_semaphore()
    for other in others:
        pl.semaphore_signal(barrier, inc=1, device_id=other, device_id_type=MESH)
    return barrier, len(others)


def silu(values):
    half = values * 0.5
    return half + half * jnp.tanh(half)


def norm(values):
    center = values - jnp.mean(values, axis=-1, keepdims=True)
    spread = jnp.mean(center * center, axis=-1, keepdims=True)
    return center * lax.rsqrt(spread + 1e-05)


def program_kernel(
    events, w_in, neg_in, lens, order, targets_in, target_ids, w_out_in, neg_ids,
    loss_out, grad_out,
    w_buf, normed, kv_st, q_st, kv_buf, q_buf, key, q_pos, q_low, total, att_st, k_from,
    heads, gate, targets, w_out, neg_rows, neg, mixed, users, wanted, stats, stats_sib,
    logits, prob, grad, ra1, rb1, sa, sb, ra2, rb2, tz, rz,
    w_sem, loc_sem, kv_ss, kv_fs, kv_rs, q_ss, q_rs, n_xs, n_ss, n_rs, a_ss, a_rs,
    u_sem, t_sem, s_sem, g_ss, g_rs, h_ss, h_rs, z_ss, z_rs,
):
    xh, z, xl, y, c = place()
    dp = lax.axis_index("dp")
    me = lax.axis_index("ctx")
    chip = me // 2
    sib = (dp, chip * 2 + 1 - c)
    xs = [(xh, 1 - xl), (1 - xh, xl), (1 - xh, 1 - xl)]
    x_peers = [device(a, z, b, y, c) for a, b in xs]
    ys = [lax.rem(y + k, 4) for k in range(1, 4)]
    y_peers = [device(xh, z, xl, b, c) for b in ys]
    zs = [lax.rem(z + k, 8) for k in range(1, 8)]
    z_peers = [device(xh, b, xl, y, c) for b in zs]
    up, down, across = z_peers[0], z_peers[6], x_peers[1]
    goes = [chip] + [(xl + a) % 2 * 4 + lax.rem(y + b, 4) for a, b in PEERS]
    comes = [chip] + [(xl + a) % 2 * 4 + lax.rem(y + 4 - b, 4) for a, b in PEERS]

    barrier, count = greet(
        x_peers[1:] + z_peers + [(dp, lax.rem(me + k, SLOTS)) for k in range(1, SLOTS)]
    )
    far = (1 - xl) * 512
    near = xl * 512
    offsets = [3072 + far, 1024 + far, 2048 + far, 3072 + near, 1024 + near, 2048 + near, 0, 512]
    w_copies = [
        pltpu.make_async_copy(
            w_in.at[:, pl.ds(pl.multiple_of(off, 512), 512)], w_buf.at[i], w_sem.at[i]
        )
        for i, off in enumerate(offsets)
    ]
    for copy in w_copies:
        copy.start()
    loads = [
        pltpu.make_async_copy(w_out_in, w_out, loc_sem.at[0]),
        pltpu.make_async_copy(targets_in, targets, loc_sem.at[1]),
    ]
    for copy in loads:
        copy.start()
    neg_rows[...] = neg_in[...].astype(F32).reshape(8, 2, 8, WIDTH)
    neg[dp] = neg_rows[:, c].reshape(64, WIDTH).astype(BF16)
    normed[...] = norm(events[...].astype(F32)).astype(BF16)
    wanted[0] = target_ids[...].astype(F32)
    pl.semaphore_wait(barrier, count)

    sends = []

    def start(copy):
        copy.start()
        sends.append(copy)

    start(remote(neg.at[dp], neg.at[dp], n_xs, n_rs.at[dp], across))
    start(remote(neg.at[dp], neg.at[dp], n_ss.at[0, 0], n_rs.at[dp], up))
    start(remote(neg.at[dp], neg.at[dp], n_ss.at[1, 0], n_rs.at[dp], down))
    t_copy = remote(wanted.at[0], wanted.at[1], t_sem.at[0], t_sem.at[1], sib)
    start(t_copy)

    def neg_wait(index):
        remote(neg.at[index], neg.at[index], n_xs, n_rs.at[index], sib).wait_recv()

    def neg_pass(index, direction, i):
        target = up if direction == 0 else down
        start(remote(neg.at[index], neg.at[index], n_ss.at[direction, i], n_rs.at[index], target))

    def ring(s, side):
        mine = xh if side == 0 else 1 - xh
        ups = mine * 8 + lax.rem(z + 8 - s, 8)
        downs = mine * 8 + lax.rem(z + s, 8)
        neg_wait(ups)
        if s > 0:
            neg_wait(downs)
        if s < 3:
            neg_pass(ups, 0, 2 * s + side)
            neg_pass(downs, 1, 2 * s + side)
        elif side == 1:
            neg_pass(lax.rem(z + 5, 8), 0, 6)
            neg_pass(8 + lax.rem(z + 3, 8), 1, 6)

    def block(i):
        w_copies[i].wait()
        return silu(jnp.dot(normed[...], w_buf[i], preferred_element_type=F32)).astype(BF16)

    def kv_send(i):
        h = goes[i]
        start(remote(kv_st.at[h], kv_buf.at[i, :, c], kv_ss.at[i], kv_rs.at[i, c], (dp, 2 * h + c)))

    def q_send(i):
        h = goes[i]
        for core in range(2):
            part = q_st.at[h, pl.ds(128 * core, 128)]
            start(remote(part, q_buf.at[i, c], q_ss.at[i, core], q_rs.at[i, c], (dp, 2 * h + core)))

    def kv_block(i, part, side):
        value = block(i)
        for k in range(4):
            kv_st[4 * side + k, part] = value[:, 128 * k : 128 * (k + 1)]

    def q_block(i, side):
        value = block(i)
        for k in range(4):
            q_st[4 * side + k] = value[:, 128 * k : 128 * (k + 1)]

    kv_block(0, 0, 1 - xl)
    kv_block(1, 1, 1 - xl)
    kv_send(1)
    q_block(2, 1 - xl)
    q_send(1)
    kv_block(3, 0, xl)
    kv_block(4, 1, xl)
    kv_send(2)
    start(remote(kv_st.at[chip], kv_buf.at[0, :, c], kv_ss.at[0], kv_rs.at[0, c], sib))
    kv_send(3)
    q_block(5, xl)
    q_send(2)
    q_send(3)
    rows_mine = pl.ds(pl.multiple_of(128 * c, 128), 128)
    rows_sib = pl.ds(pl.multiple_of(128 * (1 - c), 128), 128)
    start(remote(q_st.at[chip, rows_sib], q_buf.at[0, c], q_ss.at[0, 0], q_rs.at[0, c], sib))
    for i in (4, 5, 6, 7):
        kv_send(i)
        q_send(i)

    q_buf[0, c] = q_st[chip, rows_mine]
    kv_buf[0, 0, c] = kv_st[chip, 0]
    kv_buf[0, 1, c] = kv_st[chip, 1]
    total[...] = jnp.zeros_like(total)
    sizes = [lens[0, u] for u in range(4)]
    starts = [0, sizes[0], sizes[0] + sizes[1], sizes[0] + sizes[1] + sizes[2]]

    def pick(pos, values):
        got = jnp.where(pos >= starts[1], values[1], values[0])
        got = jnp.where(pos >= starts[2], values[2], got)
        return jnp.where(pos >= starts[3], values[3], got)

    half_row = lax.broadcasted_iota(jnp.int32, (128, HEAD), 0) + 128 * c
    col = lax.broadcasted_iota(jnp.int32, (128, HEAD), 1)
    factor = 0.5 / math.sqrt(HEAD)
    for i in range(8):
        for core in range(2):
            first = order[0, 2 * comes[i] + core] * ROWS
            k_from[2 * i + core] = first
            pos = half_row + first
            q_pos[i, core] = pos
            q_low[i, core] = pick(pos, starts)

    def tile(q, k, v, first, low, high=None):
        half = jnp.dot(q, k, preferred_element_type=F32) * factor
        weight = half + half * jnp.tanh(half)
        parts = []
        for j in range(2):
            k_pos = col + (first + HEAD * j)
            seen = k_pos >= low
            if high is not None:
                seen = seen & (k_pos <= high)
            part = weight[:, HEAD * j : HEAD * (j + 1)]
            parts.append(jnp.where(seen, part, 0.0).astype(BF16))
        return jnp.dot(jnp.concatenate(parts, axis=1), v, preferred_element_type=F32)

    def alone(i, a):
        return tile(
            q_buf[i, a], key[i, a], kv_buf[i, 1, a], k_from[2 * i + a], q_low[i, a], q_pos[i, a]
        )

    def either(i, a, j, b):
        one, two = k_from[2 * i + a], k_from[2 * j + b]
        later = one > two
        value = tile(
            jnp.where(later, q_buf[i, a], q_buf[j, b]),
            jnp.where(later, key[j, b], key[i, a]),
            jnp.where(later, kv_buf[j, 1, b], kv_buf[i, 1, a]),
            jnp.minimum(one, two),
            jnp.where(later, q_low[i, a], q_low[j, b]),
        )
        return jnp.where(later, value, 0.0), jnp.where(later, 0.0, value)

    def within(i):
        one, two = alone(i, 0), alone(i, 1)
        more = either(i, 0, i, 1)
        total[i, 0] += one + more[0]
        total[i, 1] += two + more[1]

    def between(i, j):
        got = [[either(i, a, j, b) for b in range(2)] for a in range(2)]
        for a in range(2):
            total[i, a] += got[a][0][0] + got[a][1][0]
        for b in range(2):
            total[j, b] += got[0][b][1] + got[1][b][1]

    def turn_keys(i):
        for core in range(2):
            key[i, core] = kv_buf[i, 0, core].T

    def kv_wait(i, core):
        ref = kv_buf.at[i, :, core]
        remote(ref, ref, kv_ss.at[0], kv_rs.at[i, core], sib).wait_recv()

    def q_wait(i, core):
        ref = q_buf.at[i, core]
        remote(ref, ref, q_ss.at[0, 0], q_rs.at[i, core], sib).wait_recv()

    def finish(i):
        for core in range(2):
            size = pick(q_pos[i, core], sizes).astype(F32)
            att_st[i, core] = (total[i, core] / size).astype(BF16)
        if i == 0:
            start(remote(att_st.at[0, 1 - c], heads.at[me], a_ss.at[0, 0], a_rs.at[me], sib))
            heads[me] = att_st[0, c]
        else:
            for core in range(2):
                target = (dp, 2 * comes[i] + core)
                start(
                    remote(att_st.at[i, core], heads.at[me], a_ss.at[i, core], a_rs.at[me], target)
                )

    def kv_pass(i):
        kv_wait(i, c)
        ref = kv_buf.at[i, :, c]
        start(remote(ref, ref, kv_fs.at[i], kv_rs.at[i, c], sib))

    gate[:, pl.ds(0, 512)] = block(6)
    gate[:, pl.ds(512, 512)] = block(7)
    kv_wait(0, 1 - c)
    q_wait(0, 1 - c)
    turn_keys(0)
    within(0)
    ring(0, 1)
    steps = [(1, 0), (1, 1), (2, 0), (2, 1), (3, 0), (3, 1)]
    kv_pass(1)
    for i in range(1, 8):
        if i < 7:
            kv_pass(i + 1)
        kv_wait(i, 1 - c)
        q_wait(i, 0)
        q_wait(i, 1)
        turn_keys(i)
        within(i)
        if i < 7:

            def older(j, carry, i=i):
                between(i, j)
                return carry

            lax.fori_loop(0, i, older, 0)
            ring(*steps[i - 1])
    for j in (1, 2, 3, 4, 5, 6, 0):
        between(7, j)
        finish(j)
    finish(7)

    ids = neg_ids[...].astype(F32)
    ids = jnp.concatenate([ids, jnp.zeros((112, 128), F32)], axis=0).T.reshape(8, 2, 8, 128)
    ids = jnp.where(c == 0, ids[:, 0], ids[:, 1]).reshape(64, 128)
    for copy in loads:
        copy.wait()
    neg_wait(lax.rem(z + 4, 8))
    neg_wait(8 + lax.rem(z + 4, 8))
    for k in range(1, SLOTS):
        j = lax.rem(me + k, SLOTS)
        remote(heads.at[j], heads.at[j], n_xs, a_rs.at[j], sib).wait_recv()
    for core in range(2):
        rows = pl.ds(128 * core, 128)
        attended = jnp.concatenate([heads[2 * h + core] for h in range(HEADS)], axis=1)
        mixed[rows] = (norm(attended.astype(F32)) * gate[rows].astype(F32)).astype(BF16)
    vec = events[...].astype(F32) + jnp.dot(mixed[...], w_out[...], preferred_element_type=F32)
    users[0] = vec.astype(BF16)
    u_copy = remote(users.at[0], users.at[1], u_sem.at[0], u_sem.at[1], sib)
    start(u_copy)
    scale = 1.0 / math.sqrt(WIDTH)
    pos_col = jnp.sum(users[0].astype(F32) * targets[...].astype(F32), axis=1, keepdims=True) * scale
    eye = lax.broadcasted_iota(jnp.int32, (ROWS, ROWS), 0) == lax.broadcasted_iota(
        jnp.int32, (ROWS, ROWS), 1
    )
    pos = jnp.sum(jnp.where(eye, pos_col, 0.0), axis=0, keepdims=True)

    def score(side, top):
        for d in range(0, SLOTS, 4):
            part = neg[pl.ds(d, 4)].reshape(ROWS, WIDTH)
            scores = (
                lax.dot_general(
                    part, users[side], (((1,), (1,)), ((), ())), preferred_element_type=F32
                )
                * scale
            )
            id_col = jnp.concatenate([ids[:, d + i : d + i + 1] for i in range(4)], axis=0)
            scores = jnp.where(id_col != wanted[side], scores, -jnp.inf)
            top = jnp.maximum(top, jnp.max(scores, axis=0, keepdims=True))
            logits[side, pl.ds(64 * d, ROWS)] = scores
        return top

    def weigh(side, top, whole):
        for d in range(4):
            rows = pl.ds(ROWS * d, ROWS)
            weight = jnp.exp(logits[side, rows] - top)
            logits[side, rows] = weight
            whole = whole + jnp.sum(weight, axis=0, keepdims=True)
        stats[2 * side : 2 * side + 1] = top
        stats[2 * side + 1 : 2 * side + 2] = whole

    top = score(0, pos)
    weigh(0, top, jnp.exp(pos - top))
    t_copy.wait_recv()
    u_copy.wait_recv()
    top = score(1, jnp.full((1, ROWS), -1e30, F32))
    weigh(1, top, jnp.zeros((1, ROWS), F32))
    s_copy = remote(stats, stats_sib, s_sem.at[0], s_sem.at[1], sib)
    start(s_copy)
    s_copy.wait_recv()
    for side in range(2):
        near_top, near_sum = stats[2 * side : 2 * side + 1], stats[2 * side + 1 : 2 * side + 2]
        far = 2 * (1 - side)
        far_top, far_sum = stats_sib[far : far + 1], stats_sib[far + 1 : far + 2]
        top = jnp.maximum(near_top, far_top)
        near, far = jnp.exp(near_top - top), jnp.exp(far_top - top)
        whole = near_sum * near + far_sum * far
        if side == 0:
            loss_out[...] = top + jnp.log(whole) - pos
        factor = near / whole
        for d in range(4):
            rows = pl.ds(ROWS * d, ROWS)
            prob[rows, pl.ds(ROWS * side, ROWS)] = (logits[side, rows] * factor).astype(BF16)

    def grad_block(n, a, b):
        rows = pl.ds(pl.multiple_of((a * 8 + 4 * b) * 64, 256), 256)
        sides = []
        for k in range(2):
            value = jnp.dot(
                prob[rows],
                users[:, :, pl.ds(512 * k + 256 * n, 256)].reshape(2 * ROWS, 256),
                preferred_element_type=F32,
            )
            sides.append(value.reshape(4, 2, 4, 8, 256))
        grad[n, a, pl.ds(4 * b, 4)] = jnp.concatenate(sides, axis=3).astype(BF16)

    def send_x(n, k):
        a, b = xs[k]
        start(
            remote(
                grad.at[n, a, pl.ds(0, 4), b], ra1.at[n, k], g_ss.at[n, k], g_rs.at[n, k], x_peers[k]
            )
        )

    def send_y(n, k, a):
        i = 3 + 2 * k + a
        start(
            remote(
                grad.at[n, a, pl.ds(4, 4), :, ys[k]],
                rb1.at[n, k, a],
                g_ss.at[n, i],
                g_rs.at[n, i],
                y_peers[k],
            )
        )

    for n in range(2):
        grad_block(n, 1 - xh, 0)
        send_x(n, 2)
        send_x(n, 1)
        grad_block(n, 0, 1)
        for k in (1, 0, 2):
            send_y(n, k, 0)
        grad_block(n, xh, 0)
        send_x(n, 0)
        grad_block(n, 1, 1)
        for k in (1, 0, 2):
            send_y(n, k, 1)

    def wide(ref):
        return ref[...].astype(F32)

    for n in range(2):
        for k in range(3):
            remote(ra1.at[n, k], ra1.at[n, k], g_ss.at[n, k], g_rs.at[n, k], sib).wait_recv()
        sa[n] = (
            wide(grad.at[n, xh, pl.ds(0, 4), xl]) + wide(ra1.at[n, 0]) + wide(ra1.at[n, 1]) + wide(ra1.at[n, 2])
        ).astype(BF16)
        for k in (1, 0, 2):
            start(
                remote(sa.at[n, :, ys[k]], ra2.at[n, k], h_ss.at[n, k], h_rs.at[n, k], y_peers[k])
            )
        for k in range(3):
            for a in range(2):
                ref = rb1.at[n, k, a]
                remote(ref, ref, g_ss.at[n, 0], g_rs.at[n, 3 + 2 * k + a], sib).wait_recv()
        sb[n] = (
            wide(grad.at[n, :, pl.ds(4, 4), :, y])
            + wide(rb1.at[n, 0])
            + wide(rb1.at[n, 1])
            + wide(rb1.at[n, 2])
        ).astype(BF16)
        for k in (2, 1, 0):
            a, b = xs[k]
            start(
                remote(
                    sb.at[n, a, :, b], rb2.at[n, k], h_ss.at[n, 3 + k], h_rs.at[n, 3 + k], x_peers[k]
                )
            )
    for n in range(2):
        for k in range(3):
            remote(ra2.at[n, k], ra2.at[n, k], h_ss.at[n, 0], h_rs.at[n, k], sib).wait_recv()
        tz[n, pl.ds(0, 4)] = (
            wide(sa.at[n, :, y]) + wide(ra2.at[n, 0]) + wide(ra2.at[n, 1]) + wide(ra2.at[n, 2])
        ).astype(BF16)
        for k in range(3):
            remote(rb2.at[n, k], rb2.at[n, k], h_ss.at[n, 0], h_rs.at[n, 3 + k], sib).wait_recv()
        tz[n, pl.ds(4, 4)] = (
            wide(sb.at[n, xh, :, xl]) + wide(rb2.at[n, 0]) + wide(rb2.at[n, 1]) + wide(rb2.at[n, 2])
        ).astype(BF16)
        for k in (3, 2, 4, 1, 5, 0, 6):
            start(remote(tz.at[n, zs[k]], rz.at[n, k], z_ss.at[n, k], z_rs.at[n, k], z_peers[k]))
    for n in range(2):
        result = tz[n, z].astype(F32)
        for k in range(7):
            remote(rz.at[n, k], rz.at[n, k], z_ss.at[n, 0], z_rs.at[n, k], sib).wait_recv()
            result = result + rz[n, k].astype(F32)
        result = result * scale
        grad_out[:, pl.ds(256 * n, 256)] = result[:8]
        grad_out[:, pl.ds(512 + 256 * n, 256)] = result[8:]
    for copy in sends:
        copy.wait_send()


def shards(events, w_in, w_out, targets, target_ids, lengths, block_order, negatives, neg_ids):
    any_space = pl.BlockSpec(memory_space=pl.ANY)
    vmem = pl.BlockSpec(memory_space=pltpu.VMEM)
    smem = pl.BlockSpec(memory_space=pltpu.SMEM)
    dma = pltpu.SemaphoreType.DMA
    loss, grad = pl.pallas_call(
        program_kernel,
        out_shape=(
            jax.ShapeDtypeStruct((1, ROWS), F32),
            jax.ShapeDtypeStruct((8, WIDTH), F32),
        ),
        in_specs=[vmem, any_space, vmem, smem, smem, any_space, vmem, any_space, vmem],
        out_specs=(vmem, vmem),
        scratch_shapes=[
            pltpu.VMEM((8, WIDTH, 512), BF16),
            pltpu.VMEM((ROWS, WIDTH), BF16),
            pltpu.VMEM((HEADS, 2, ROWS, HEAD), BF16),
            pltpu.VMEM((HEADS, ROWS, HEAD), BF16),
            pltpu.VMEM((8, 2, 2, ROWS, HEAD), BF16),
            pltpu.VMEM((8, 2, 128, HEAD), BF16),
            pltpu.VMEM((8, 2, HEAD, ROWS), BF16),
            pltpu.VMEM((8, 2, 128, HEAD), jnp.int32),
            pltpu.VMEM((8, 2, 128, HEAD), jnp.int32),
            pltpu.VMEM((8, 2, 128, HEAD), F32),
            pltpu.VMEM((8, 2, 128, HEAD), BF16),
            pltpu.SMEM((SLOTS,), jnp.int32),
            pltpu.VMEM((SLOTS, 128, HEAD), BF16),
            pltpu.VMEM((ROWS, WIDTH), BF16),
            pltpu.VMEM((ROWS, WIDTH), BF16),
            pltpu.VMEM((WIDTH, WIDTH), BF16),
            pltpu.VMEM((8, 2, 8, WIDTH), F32),
            pltpu.VMEM((SLOTS, 64, WIDTH), BF16),
            pltpu.VMEM((ROWS, WIDTH), BF16),
            pltpu.VMEM((2, ROWS, WIDTH), BF16),
            pltpu.VMEM((2, 1, ROWS), F32),
            pltpu.VMEM((8, ROWS), F32),
            pltpu.VMEM((8, ROWS), F32),
            pltpu.VMEM((2, 1024, ROWS), F32),
            pltpu.VMEM((1024, 2 * ROWS), BF16),
            pltpu.VMEM((2, 2, 8, 2, 4, 16, 256), BF16),
            pltpu.VMEM((2, 3, 4, 4, 16, 256), BF16),
            pltpu.VMEM((2, 3, 2, 4, 2, 16, 256), BF16),
            pltpu.VMEM((2, 4, 4, 16, 256), BF16),
            pltpu.VMEM((2, 2, 4, 2, 16, 256), BF16),
            pltpu.VMEM((2, 3, 4, 16, 256), BF16),
            pltpu.VMEM((2, 3, 4, 16, 256), BF16),
            pltpu.VMEM((2, 8, 16, 256), BF16),
            pltpu.VMEM((2, 7, 16, 256), BF16),
            dma((8,)),
            dma((2,)),
            dma((8,)),
            dma((8,)),
            dma((8, 2)),
            dma((8, 2)),
            dma((8, 2)),
            dma,
            dma((2, 7)),
            dma((SLOTS,)),
            dma((8, 2)),
            dma((SLOTS,)),
            dma((2,)),
            dma((2,)),
            dma((2,)),
            dma((2, 9)),
            dma((2, 9)),
            dma((2, 6)),
            dma((2, 6)),
            dma((2, 7)),
            dma((2, 7)),
        ],
        compiler_params=pltpu.CompilerParams(
            collective_id=1, has_side_effects=True, vmem_limit_bytes=VMEM_LIMIT
        ),
        name="program",
    )(
        events, w_in, negatives, lengths, block_order, targets, target_ids.reshape(1, ROWS), w_out,
        neg_ids.reshape(SLOTS, 128),
    )
    return (loss.reshape(ROWS), grad)


def solution(mesh):
    return jax.shard_map(
        shards,
        mesh=mesh,
        in_specs=(
            P(("dp", "ctx"), None),
            P(),
            P(),
            P(("dp", "ctx"), None),
            P(("dp", "ctx")),
            P("dp", None),
            P("dp", None),
            P("dp", None),
            P(),
        ),
        out_specs=(P(("dp", "ctx")), P(("dp", "ctx"), None)),
        check_vma=False,
    )
```

time: 91.5 us -> 81.2 us (0.89)
  Pallas kernels: 87.2 us -> 76.8 us
    pallas_call x3 -> x1, Pallas kernels: 87.2 us -> 76.8 us  [shards(): pl.pallas_call(program_kernel, out_shape=(jax.ShapeDtypeStruct((1, ROWS),...]
where the time goes in v3:
time: 81.2 us; the launch traced here: 80.1 us
  Pallas kernels  76.8 us (95%)
  local copies, waits for them, and re-layouts  2.6 us (3%)
    pallas_call x1, Pallas kernels, shards(): pl.pallas_call(program_kernel, out_shape=(jax.ShapeDtypeStruct((1, ROWS),...  76.8 us
    unnamed x2, local copies, waits for them, and re-layouts  2.6 us

profile of v3, /device:TPU:24, one launch (start us, length us, event | category | flops | bytes accessed | tf_op | source)
XLA Modules:
  0.0 80.1 jit_solution(12278435323830781838)
XLA Ops:
  0.6 76.8 %program.1 = (f32[1,256]{1,0:T(1,128)}, f32[8,1024]{1,0:T(8,128)}) custom-call(bf16[256,1024]{1,0:T(8,128)(2,1)} %events.1, bf16[1024,4096]{1,0:T(8,128)(2,1)} %w_in.1, bf16[128,1024]{1,0:T(8,128)(2,1)} %neg_in.1, s32[1,4]{1,0:T(1,128)} %lens.1, s32[1,16]{1,0:T(1,128)} %order.1, bf16[256,1024]{1,0:T(8,128)(2,1)} %targets_in.1, s32[1,256]{1,0:T(1,128)} %bitcast.4, ...), custom_call_target="tpu_custom_call" | custom-call | tf_op jit(solution)/shard_map/program/pallas_call | solution.py:485
  77.5 1.2 %copy.13 = f32[256]{0:T(256)} copy(f32[256]{0:T(256)} %bitcast.5) | data formatting | bytes 2048
  78.7 1.4 %copy.14 = f32[8,1024]{1,0:T(8,128)} copy(f32[8,1024]{1,0:T(8,128)} %get-tuple-element.9) | data formatting | bytes 65536

commit v4 on v3

--- a/solution.py
+++ b/solution.py
@@ -56,7 +56,7 @@
     loss_out, grad_out,
     w_buf, normed, kv_st, q_st, kv_buf, q_buf, key, q_pos, q_low, total, att_st, k_from,
     heads, gate, targets, w_out, neg_rows, neg, mixed, users, wanted, stats, stats_sib,
-    logits, prob, grad, ra1, rb1, sa, sb, ra2, rb2, tz, rz,
+    logits, prob, grad, ta, tb, ra1, rb1, sa, sb, ra2, rb2, tz, rz,
     w_sem, loc_sem, kv_ss, kv_fs, kv_rs, q_ss, q_rs, n_xs, n_ss, n_rs, a_ss, a_rs,
     u_sem, t_sem, s_sem, g_ss, g_rs, h_ss, h_rs, z_ss, z_rs,
 ):
@@ -282,7 +282,7 @@
     turn_keys(0)
     within(0)
     ring(0, 1)
-    steps = [(1, 0), (1, 1), (2, 0), (2, 1), (3, 0), (3, 1)]
+    steps = {1: [(1, 0)], 2: [(1, 1)], 4: [(2, 0)], 5: [(2, 1)], 6: []}
     kv_pass(1)
     for i in range(1, 8):
         if i < 7:
@@ -299,19 +299,20 @@
                 return carry
 
             lax.fori_loop(0, i, older, 0)
-            ring(*steps[i - 1])
+            for step in steps.get(i, []):
+                ring(*step)
     for j in (1, 2, 3, 4, 5, 6, 0):
         between(7, j)
         finish(j)
     finish(7)
+    ring(3, 0)
+    ring(3, 1)
 
     ids = neg_ids[...].astype(F32)
     ids = jnp.concatenate([ids, jnp.zeros((112, 128), F32)], axis=0).T.reshape(8, 2, 8, 128)
     ids = jnp.where(c == 0, ids[:, 0], ids[:, 1]).reshape(64, 128)
     for copy in loads:
         copy.wait()
-    neg_wait(lax.rem(z + 4, 8))
-    neg_wait(8 + lax.rem(z + 4, 8))
     for k in range(1, SLOTS):
         j = lax.rem(me + k, SLOTS)
         remote(heads.at[j], heads.at[j], n_xs, a_rs.at[j], sib).wait_recv()
@@ -329,6 +330,9 @@
         jnp.int32, (ROWS, ROWS), 1
     )
     pos = jnp.sum(jnp.where(eye, pos_col, 0.0), axis=0, keepdims=True)
+
+    neg_wait(lax.rem(z + 4, 8))
+    neg_wait(8 + lax.rem(z + 4, 8))
 
     def score(side, top):
         for d in range(0, SLOTS, 4):
@@ -389,61 +393,117 @@
             sides.append(value.reshape(4, 2, 4, 8, 256))
         grad[n, a, pl.ds(4 * b, 4)] = jnp.concatenate(sides, axis=3).astype(BF16)
 
-    def send_x(n, k):
-        a, b = xs[k]
+    ring_x = [lax.rem(2 * xh + xl + k, 4) for k in range(4)]
+    ring_y = [lax.rem(y + k, 4) for k in range(4)]
+    x_side = [device(p // 2, z, p % 2, y, c) for p in (ring_x[1], ring_x[3])]
+    y_side = [device(xh, z, xl, p, c) for p in (ring_y[1], ring_y[3])]
+
+    def part_a(n, k, half):
+        p = ring_x[k]
+        return grad.at[n, p // 2, pl.ds(2 * half, 2), p % 2]
+
+    def part_b(n, k, half):
+        return grad.at[n, half, pl.ds(4, 4), :, ring_y[k]]
+
+    def first_a(n, way):
         start(
             remote(
-                grad.at[n, a, pl.ds(0, 4), b], ra1.at[n, k], g_ss.at[n, k], g_rs.at[n, k], x_peers[k]
+                part_a(n, 2, way), ta.at[n, way], g_ss.at[n, way], g_rs.at[n, way], x_side[way]
             )
         )
 
-    def send_y(n, k, a):
-        i = 3 + 2 * k + a
+    def plain_a(n, way):
+        half = 1 - way
         start(
             remote(
-                grad.at[n, a, pl.ds(4, 4), :, ys[k]],
-                rb1.at[n, k, a],
-                g_ss.at[n, i],
-                g_rs.at[n, i],
-                y_peers[k],
+                part_a(n, 1 + 2 * way, half),
+                ra1.at[n, way, pl.ds(2 * half, 2)],
+                g_ss.at[n, 2 + way],
+                g_rs.at[n, 2 + way],
+                x_side[way],
+            )
+        )
+
+    def first_b(n, way):
+        start(
+            remote(
+                part_b(n, 2, way), tb.at[n, way], g_ss.at[n, 6 + way], g_rs.at[n, 6 + way], y_side[way]
+            )
+        )
+
+    def plain_b(n, way):
+        half = 1 - way
+        start(
+            remote(
+                part_b(n, 1 + 2 * way, half),
+                rb1.at[n, way, half],
+                g_ss.at[n, 8 + way],
+                g_rs.at[n, 8 + way],
+                y_side[way],
             )
         )
 
     for n in range(2):
         grad_block(n, 1 - xh, 0)
-        send_x(n, 2)
-        send_x(n, 1)
+        first_a(n, 0)
+        first_a(n, 1)
         grad_block(n, 0, 1)
-        for k in (1, 0, 2):
-            send_y(n, k, 0)
+        first_b(n, 0)
+        grad_block(n, 1, 1)
+        first_b(n, 1)
+        plain_b(n, 0)
+        plain_b(n, 1)
         grad_block(n, xh, 0)
-        send_x(n, 0)
-        grad_block(n, 1, 1)
-        for k in (1, 0, 2):
-            send_y(n, k, 1)
+        plain_a(n, 0)
+        plain_a(n, 1)
 
     def wide(ref):
         return ref[...].astype(F32)
 
+    def arrive(ref, sem):
+        remote(ref, ref, n_xs, sem, sib).wait_recv()
+
     for n in range(2):
-        for k in range(3):
-            remote(ra1.at[n, k], ra1.at[n, k], g_ss.at[n, k], g_rs.at[n, k], sib).wait_recv()
+        for way in range(2):
+            arrive(ta.at[n, way], g_rs.at[n, way])
+            ta[n, way] = (wide(ta.at[n, way]) + wide(part_a(n, 1 + 2 * way, way))).astype(BF16)
+            start(
+                remote(
+                    ta.at[n, way],
+                    ra1.at[n, way, pl.ds(2 * way, 2)],
+                    g_ss.at[n, 4 + way],
+                    g_rs.at[n, 4 + way],
+                    x_side[way],
+                )
+            )
+        for way in range(2):
+            arrive(tb.at[n, way], g_rs.at[n, 6 + way])
+            tb[n, way] = (wide(tb.at[n, way]) + wide(part_b(n, 1 + 2 * way, way))).astype(BF16)
+            start(
+                remote(
+                    tb.at[n, way],
+                    rb1.at[n, way, way],
+                    g_ss.at[n, 10 + way],
+                    g_rs.at[n, 10 + way],
+                    y_side[way],
+                )
+            )
+    for n in range(2):
+        for way in range(2):
+            arrive(ra1.at[n, way, pl.ds(2 - 2 * way, 2)], g_rs.at[n, 2 + way])
+            arrive(ra1.at[n, way, pl.ds(2 * way, 2)], g_rs.at[n, 4 + way])
         sa[n] = (
-            wide(grad.at[n, xh, pl.ds(0, 4), xl]) + wide(ra1.at[n, 0]) + wide(ra1.at[n, 1]) + wide(ra1.at[n, 2])
+            wide(grad.at[n, xh, pl.ds(0, 4), xl]) + wide(ra1.at[n, 0]) + wide(ra1.at[n, 1])
         ).astype(BF16)
         for k in (1, 0, 2):
             start(
                 remote(sa.at[n, :, ys[k]], ra2.at[n, k], h_ss.at[n, k], h_rs.at[n, k], y_peers[k])
             )
-        for k in range(3):
-            for a in range(2):
-                ref = rb1.at[n, k, a]
-                remote(ref, ref, g_ss.at[n, 0], g_rs.at[n, 3 + 2 * k + a], sib).wait_recv()
+        for way in range(2):
+            arrive(rb1.at[n, way, 1 - way], g_rs.at[n, 8 + way])
+            arrive(rb1.at[n, way, way], g_rs.at[n, 10 + way])
         sb[n] = (
-            wide(grad.at[n, :, pl.ds(4, 4), :, y])
-            + wide(rb1.at[n, 0])
-            + wide(rb1.at[n, 1])
-            + wide(rb1.at[n, 2])
+            wide(grad.at[n, :, pl.ds(4, 4), :, y]) + wide(rb1.at[n, 0]) + wide(rb1.at[n, 1])
         ).astype(BF16)
         for k in (2, 1, 0):
             a, b = xs[k]
@@ -475,6 +535,11 @@
         grad_out[:, pl.ds(512 + 256 * n, 256)] = result[8:]
     for copy in sends:
         copy.wait_send()
+
+
+def hand_over_kernel(loss_in, grad_in, loss_out, grad_out):
+    loss_out[...] = loss_in[...]
+    grad_out[...] = grad_in[...]
 
 
 def shards(events, w_in, w_out, targets, target_ids, lengths, block_order, negatives, neg_ids):
@@ -517,8 +582,10 @@
             pltpu.VMEM((2, 1024, ROWS), F32),
             pltpu.VMEM((1024, 2 * ROWS), BF16),
             pltpu.VMEM((2, 2, 8, 2, 4, 16, 256), BF16),
-            pltpu.VMEM((2, 3, 4, 4, 16, 256), BF16),
-            pltpu.VMEM((2, 3, 2, 4, 2, 16, 256), BF16),
+            pltpu.VMEM((2, 2, 2, 4, 16, 256), BF16),
+            pltpu.VMEM((2, 2, 4, 2, 16, 256), BF16),
+            pltpu.VMEM((2, 2, 4, 4, 16, 256), BF16),
+            pltpu.VMEM((2, 2, 2, 4, 2, 16, 256), BF16),
             pltpu.VMEM((2, 4, 4, 16, 256), BF16),
             pltpu.VMEM((2, 2, 4, 2, 16, 256), BF16),
             pltpu.VMEM((2, 3, 4, 16, 256), BF16),
@@ -540,8 +607,8 @@
             dma((2,)),
             dma((2,)),
             dma((2,)),
-            dma((2, 9)),
-            dma((2, 9)),
+            dma((2, 12)),
+            dma((2, 12)),
             dma((2, 6)),
             dma((2, 6)),
             dma((2, 7)),
@@ -555,6 +622,16 @@
         events, w_in, negatives, lengths, block_order, targets, target_ids.reshape(1, ROWS), w_out,
         neg_ids.reshape(SLOTS, 128),
     )
+    loss, grad = pl.pallas_call(
+        hand_over_kernel,
+        out_shape=(
+            jax.ShapeDtypeStruct((1, ROWS), F32),
+            jax.ShapeDtypeStruct((8, WIDTH), F32),
+        ),
+        in_specs=[vmem, vmem],
+        out_specs=(vmem, vmem),
+        name="hand_over",
+    )(loss, grad)
     return (loss.reshape(ROWS), grad)
 
 

time: 81.2 us -> 76.8 us (0.946); the launches traced: 80.1 us -> 76.6 us
  local copies, waits for them, and re-layouts: 2.6 us -> 0 us
    unnamed x2 -> x0, local copies, waits for them, and re-layouts: 2.6 us -> none
    pallas_call x1, Pallas kernels: 76.8 us -> 74.6 us  [shards(): pl.pallas_call(program_kernel, out_shape=(jax.ShapeDtypeStruct((1, ROWS),...]
    pallas_call x0 -> x1, Pallas kernels: none -> 1.38 us  [shards(): pl.pallas_call(hand_over_kernel, out_shape=(jax.ShapeDtypeStruct((1, ROWS...]
where the time goes in v4:
time: 76.8 us; the launch traced here: 76.6 us
  Pallas kernels  76 us (99%)
    pallas_call x1, Pallas kernels, shards(): pl.pallas_call(program_kernel, out_shape=(jax.ShapeDtypeStruct((1, ROWS),...  74.6 us

profile of v4, /device:TPU:24, one launch (start us, length us, event | category | flops | bytes accessed | tf_op | source)
XLA Modules:
  0.0 76.6 jit_solution(3479501699190399336)
XLA Ops:
  0.6 74.6 %program.1 = (f32[1,256]{1,0:T(1,128)}, f32[8,1024]{1,0:T(8,128)}) custom-call(bf16[256,1024]{1,0:T(8,128)(2,1)} %events.1, bf16[1024,4096]{1,0:T(8,128)(2,1)} %w_in.1, bf16[128,1024]{1,0:T(8,128)(2,1)} %neg_in.1, s32[1,4]{1,0:T(1,128)} %lens.1, s32[1,16]{1,0:T(1,128)} %order.1, bf16[256,1024]{1,0:T(8,128)(2,1)} %targets_in.1, s32[1,256]{1,0:T(1,128)} %bitcast.4, ...), custom_call_target="tpu_custom_call" | custom-call | tf_op jit(solution)/shard_map/program/pallas_call | solution.py:550
  75.3 1.4 %hand_over.1 = (f32[1,256]{1,0:T(1,128)}, f32[8,1024]{1,0:T(8,128)}) custom-call(f32[1,256]{1,0:T(1,128)} %get-tuple-element.6.loss_in, f32[8,1024]{1,0:T(8,128)} %get-tuple-element.7.grad_in), custom_call_target="tpu_custom_call" | custom-call | tf_op jit(solution)/shard_map/hand_over/pallas_call | solution.py:625

commit v5 on v4

--- a/solution.py
+++ b/solution.py
@@ -75,9 +75,6 @@
     goes = [chip] + [(xl + a) % 2 * 4 + lax.rem(y + b, 4) for a, b in PEERS]
     comes = [chip] + [(xl + a) % 2 * 4 + lax.rem(y + 4 - b, 4) for a, b in PEERS]
 
-    barrier, count = greet(
-        x_peers[1:] + z_peers + [(dp, lax.rem(me + k, SLOTS)) for k in range(1, SLOTS)]
-    )
     far = (1 - xl) * 512
     near = xl * 512
     offsets = [3072 + far, 1024 + far, 2048 + far, 3072 + near, 1024 + near, 2048 + near, 0, 512]
@@ -89,15 +86,18 @@
     ]
     for copy in w_copies:
         copy.start()
+    barrier, count = greet(
+        x_peers[1:] + z_peers + [(dp, lax.rem(me + k, SLOTS)) for k in range(1, SLOTS)]
+    )
     loads = [
         pltpu.make_async_copy(w_out_in, w_out, loc_sem.at[0]),
         pltpu.make_async_copy(targets_in, targets, loc_sem.at[1]),
     ]
     for copy in loads:
         copy.start()
+    normed[...] = norm(events[...].astype(F32)).astype(BF16)
     neg_rows[...] = neg_in[...].astype(F32).reshape(8, 2, 8, WIDTH)
     neg[dp] = neg_rows[:, c].reshape(64, WIDTH).astype(BF16)
-    normed[...] = norm(events[...].astype(F32)).astype(BF16)
     wanted[0] = target_ids[...].astype(F32)
     pl.semaphore_wait(barrier, count)
 
@@ -355,22 +355,24 @@
             weight = jnp.exp(logits[side, rows] - top)
             logits[side, rows] = weight
             whole = whole + jnp.sum(weight, axis=0, keepdims=True)
-        stats[2 * side : 2 * side + 1] = top
-        stats[2 * side + 1 : 2 * side + 2] = whole
+        stats[side, 0:1] = top
+        stats[side, 1:2] = whole
+        copy = remote(
+            stats.at[side], stats_sib.at[1 - side], s_sem.at[0, side], s_sem.at[1, side], sib
+        )
+        start(copy)
+        return copy
 
     top = score(0, pos)
-    weigh(0, top, jnp.exp(pos - top))
+    one = weigh(0, top, jnp.exp(pos - top))
     t_copy.wait_recv()
     u_copy.wait_recv()
     top = score(1, jnp.full((1, ROWS), -1e30, F32))
-    weigh(1, top, jnp.zeros((1, ROWS), F32))
-    s_copy = remote(stats, stats_sib, s_sem.at[0], s_sem.at[1], sib)
-    start(s_copy)
-    s_copy.wait_recv()
-    for side in range(2):
-        near_top, near_sum = stats[2 * side : 2 * side + 1], stats[2 * side + 1 : 2 * side + 2]
-        far = 2 * (1 - side)
-        far_top, far_sum = stats_sib[far : far + 1], stats_sib[far + 1 : far + 2]
+    two = weigh(1, top, jnp.zeros((1, ROWS), F32))
+    for side, copy in ((1, one), (0, two)):
+        copy.wait_recv()
+        near_top, near_sum = stats[side, 0:1], stats[side, 1:2]
+        far_top, far_sum = stats_sib[side, 0:1], stats_sib[side, 1:2]
         top = jnp.maximum(near_top, far_top)
         near, far = jnp.exp(near_top - top), jnp.exp(far_top - top)
         whole = near_sum * near + far_sum * far
@@ -463,6 +465,12 @@
     def arrive(ref, sem):
         remote(ref, ref, n_xs, sem, sib).wait_recv()
 
+    def drain(keep):
+        while len(sends) > keep:
+            sends.pop(0).wait_send()
+
+    drain(16)
+
     for n in range(2):
         for way in range(2):
             arrive(ta.at[n, way], g_rs.at[n, way])
@@ -515,6 +523,7 @@
     for n in range(2):
         for k in range(3):
             remote(ra2.at[n, k], ra2.at[n, k], h_ss.at[n, 0], h_rs.at[n, k], sib).wait_recv()
+        drain(12)
         tz[n, pl.ds(0, 4)] = (
             wide(sa.at[n, :, y]) + wide(ra2.at[n, 0]) + wide(ra2.at[n, 1]) + wide(ra2.at[n, 2])
         ).astype(BF16)
@@ -525,6 +534,7 @@
         ).astype(BF16)
         for k in (3, 2, 4, 1, 5, 0, 6):
             start(remote(tz.at[n, zs[k]], rz.at[n, k], z_ss.at[n, k], z_rs.at[n, k], z_peers[k]))
+    drain(14)
     for n in range(2):
         result = tz[n, z].astype(F32)
         for k in range(7):
@@ -577,8 +587,8 @@
             pltpu.VMEM((ROWS, WIDTH), BF16),
             pltpu.VMEM((2, ROWS, WIDTH), BF16),
             pltpu.VMEM((2, 1, ROWS), F32),
-            pltpu.VMEM((8, ROWS), F32),
-            pltpu.VMEM((8, ROWS), F32),
+            pltpu.VMEM((2, 8, ROWS), F32),
+            pltpu.VMEM((2, 8, ROWS), F32),
             pltpu.VMEM((2, 1024, ROWS), F32),
             pltpu.VMEM((1024, 2 * ROWS), BF16),
             pltpu.VMEM((2, 2, 8, 2, 4, 16, 256), BF16),
@@ -606,7 +616,7 @@
             dma((SLOTS,)),
             dma((2,)),
             dma((2,)),
-            dma((2,)),
+            dma((2, 2)),
             dma((2, 12)),
             dma((2, 12)),
             dma((2, 6)),

time: 76.8 us -> 76.6 us (level)
  no operation moved by 1% of the time
where the time goes in v5:
time: 76.6 us; the launch traced here: 76.4 us
  Pallas kernels  75.8 us (99%)
    pallas_call x1, Pallas kernels, shards(): pl.pallas_call(program_kernel, out_shape=(jax.ShapeDtypeStruct((1, ROWS),...  74.4 us

profile of v5, /device:TPU:24, one launch (start us, length us, event | category | flops | bytes accessed | tf_op | source)
XLA Modules:
  0.0 76.4 jit_solution(16168713651103487818)
XLA Ops:
  0.6 74.4 %program.1 = (f32[1,256]{1,0:T(1,128)}, f32[8,1024]{1,0:T(8,128)}) custom-call(bf16[256,1024]{1,0:T(8,128)(2,1)} %events.1, bf16[1024,4096]{1,0:T(8,128)(2,1)} %w_in.1, bf16[128,1024]{1,0:T(8,128)(2,1)} %neg_in.1, s32[1,4]{1,0:T(1,128)} %lens.1, s32[1,16]{1,0:T(1,128)} %order.1, bf16[256,1024]{1,0:T(8,128)(2,1)} %targets_in.1, s32[1,256]{1,0:T(1,128)} %bitcast.4, ...), custom_call_target="tpu_custom_call" | custom-call | tf_op jit(solution)/shard_map/program/pallas_call | solution.py:560
  75.1 1.4 %hand_over.1 = (f32[1,256]{1,0:T(1,128)}, f32[8,1024]{1,0:T(8,128)}) custom-call(f32[1,256]{1,0:T(1,128)} %get-tuple-element.6.loss_in, f32[8,1024]{1,0:T(8,128)} %get-tuple-element.7.grad_in), custom_call_target="tpu_custom_call" | custom-call | tf_op jit(solution)/shard_map/hand_over/pallas_call | solution.py:635
